TPU v7x, 32 devices: a whole 2x2x4 slice. The times are simulated.
32 devices in a mesh: groups: 2 (over x), tile: 16 (over z, y, core).
Axes of the slice: x: 2, y: 2, z: 4, core: 2. Of those that a mesh axis runs over, the one named last changes fastest.
Arguments:
- spectrum: float32 [40, 36, 32, 128], P(None, None, ('groups', 'tile')), parts along dimension 2, may hold values from 0 to 1
- sea_mask: int32 [32, 128], P(('groups', 'tile')), parts along dimension 0, may hold values from 0 to 1, as said below
- card_deal: int32 [32, 128], P(('groups', 'tile')), parts along dimension 0, may hold values from -1 to 255, as said below
- wind: float32 [2, 32, 128], P(None, ('groups', 'tile')), parts along dimension 1, may hold values from -5 to 5
Outputs:
- spectrum_out: float32 [40, 36, 32, 128], P(None, None, ('groups', 'tile')), parts along dimension 2
- card_energy: float32 [512], P(('groups', 'tile')), parts along dimension 0
There are 2 independent parts, one for each index of `groups`. A program takes and returns all parts, laid end to end along the dimension named above; each array names one. Nothing has to cross between parts.
Inputs may be any that keep to these rules, and one draw needn't show every extreme that they name: `sea_mask`: each row is sea (1) from its first cell up to a coastline and land (0) beyond. One tile of 1 row, placed by the seed, is all sea; the other tiles hold 8 times q or q + 1 sea points each, q = r // 15 with r = 16 (8) / 8, so that the window holds 256 sea points; within a tile the rows' sea counts differ by at most one, the first rows holding more. `card_deal`: land cells hold -1. Sea cells, numbered i = 0, 1, ... in row-major order over the window, hold c * 16 + s with card c = (i + o) mod 16 for an offset o drawn from the seed and slot s = i // 16. Every card holds exactly 16 points, and at most 8 points of one tile, a count that the all-sea tile reaches on every card.
All inputs are finite; a program needn't handle non-finite values.
Results may differ from a plain program's by a relative error of at most 0.0001.
Values sent between devices are 32-bit elements; how exact they have to be, the bound alone decides.
No kernel may reach another device: no remote copies, remote signals or barrier semaphores. Data moves between devices by JAX's collectives and lax.ppermute only.
A program may use at most 64 MiB of HBM per device.

v0:
```python
import functools
import math

import jax
import jax.numpy as jnp
import numpy as np
from jax import lax
from jax.experimental import pallas as pl
from jax.experimental.pallas import tpu as pltpu
from jax.sharding import PartitionSpec as P

STEPS = 2
SUB = 8
COURANT_TOP = 0.7
WIND_RATE = 0.15
DECAY_RATE = 0.3
QUAD_RATE = 0.5
LIMITER = 0.25
ANGLE_UP = -11.48
ANGLE_DOWN = 33.56
SHIFT_UP = math.log(1.25) / math.log(1.1)
SHIFT_DOWN = math.log(0.75) / math.log(1.1)
GAIN_UP = 1.25 ** (-4)
GAIN_DOWN = 0.75 ** (-4)
GAIN_BOTH = 0.9375 ** (-4)

LANES = 128
ROWS = 8
PAD = 4


def split(offset):
    base = math.floor(offset)
    return base, offset - base


GAIN = 2.0 * GAIN_BOTH / (GAIN_UP * GAIN_DOWN)
UP_K, UP_W = split(SHIFT_UP)
DOWN_K, DOWN_W = split(SHIFT_DOWN)


def directions(count):
    angles = 2.0 * math.pi * np.arange(count) / count
    return np.cos(angles), np.sin(angles)


def tables(freq_count, dir_count):
    levels = 3.0 ** (np.arange(freq_count) / (freq_count - 1))
    speeds = COURANT_TOP * 1.1 ** (-np.arange(freq_count, dtype=np.float64))
    up_j, up_z = split(ANGLE_UP * dir_count / 360.0)
    near_up = max(up_z, 1.0 - up_z)
    rate = (1.0 - UP_W) * near_up / LIMITER
    rows = [
        speeds,
        rate * QUAD_RATE * GAIN * GAIN * levels,
        GAIN / LIMITER * WIND_RATE * 0.5 * levels,
        GAIN / (dir_count * np.sum(levels)) * levels,
        GAIN / LIMITER * DECAY_RATE * levels,
    ]
    return np.broadcast_to(
        np.stack(rows)[:, :, None], (len(rows), freq_count, LANES)
    ).astype(np.float32)


def pack_order(dir_count, freq_count, forward):
    cosines, _ = directions(dir_count)
    chosen = [j for j in range(dir_count) if (cosines[j] > 0) == forward]
    return [(j, kb) for j in chosen for kb in range(freq_count // ROWS)]


def pack_rows(dir_count, freq_count, edge):
    most = max(len(pack_order(dir_count, freq_count, f)) for f in (True, False))
    per = LANES // edge
    return -(-most // per) * ROWS


def pack(fetch, order, edge, lane):
    per = LANES // edge
    out = []
    for start in range(0, len(order), per):
        total = None
        for b, item in enumerate(order[start:start + per]):
            value = fetch(*item)
            if b == 0:
                total = value
            else:
                total = jnp.where(lane // edge == b, pltpu.roll(value, edge * b, 1), total)
        out.append(total)
    return out


def store_packs(fetch, pair_ref, next_ref, parity, freq_count, dir_count, edge, lane):
    for forward in (True, False):
        packs = pack(fetch, pack_order(dir_count, freq_count, forward), edge, lane)
        to_pair = parity == (0 if forward else 1)

        @pl.when(to_pair)
        def _():
            for g, value in enumerate(packs):
                pair_ref[pl.ds(g * ROWS, ROWS), :] = value

        @pl.when(jnp.logical_not(to_pair))
        def _():
            for g, value in enumerate(packs):
                next_ref[pl.ds(g * ROWS, ROWS), :] = value


def edges_kernel(freq_count, dir_count, edge, parity_ref, in_ref, mask_ref, pair_ref, next_ref):
    lane = lax.broadcasted_iota(jnp.int32, (ROWS, LANES), 1)
    mask = mask_ref[...].astype(jnp.float32)

    def fetch(j, kb):
        return in_ref[pl.ds(kb * ROWS * dir_count + j, ROWS, stride=dir_count), :] * mask

    store_packs(fetch, pair_ref, next_ref, parity_ref[0], freq_count, dir_count, edge, lane)


def step_kernel(
    freq_count, dir_count, edge, first, last,
    parity_ref, in_ref, mask_ref, wind_ref, table_ref, pair_ref, next_ref, *rest
):
    if last:
        deal_ref, out_ref, energy_ref = rest[:3]
        rest = rest[3:]
    else:
        out_ref, pair_out, next_out = rest[:3]
        rest = rest[3:]
    e_ref, u_ref, d_ref, n_ref, w_ref, acc_ref, c_ref, back_ref = rest
    blocks = freq_count // ROWS
    cosines, sines = directions(dir_count)
    lane = lax.broadcasted_iota(jnp.int32, (ROWS, LANES), 1)
    mask = mask_ref[...].astype(jnp.float32)
    half = mask * (1.0 / GAIN)
    parity = parity_ref[0]

    zero = jnp.zeros((PAD, LANES), jnp.float32)
    for j in range(dir_count):
        for ref in (e_ref, u_ref, d_ref):
            ref[j, pl.ds(0, PAD), :] = zero
            ref[j, pl.ds(PAD + freq_count, PAD), :] = zero

    @pl.when(parity == 0)
    def _():
        back_ref[0] = next_ref[...]
        back_ref[1] = pair_ref[...]

    @pl.when(parity == 1)
    def _():
        back_ref[0] = pair_ref[...]
        back_ref[1] = next_ref[...]

    place = {}
    for forward in (True, False):
        for i, item in enumerate(pack_order(dir_count, freq_count, forward)):
            place[item] = (0 if forward else 1, i)
    per = LANES // edge
    for kb in range(blocks):
        speed = table_ref[0, pl.ds(kb * ROWS, ROWS), :]
        drive_rate = table_ref[2, pl.ds(kb * ROWS, ROWS), :]
        total = jnp.zeros((ROWS, LANES), jnp.float32)
        for j in range(dir_count):
            if first:
                here = in_ref[pl.ds(kb * ROWS * dir_count + j, ROWS, stride=dir_count), :] * mask
            else:
                here = in_ref[j, pl.ds(kb * ROWS, ROWS), :]
            side, i = place[(j, kb)]
            beside = back_ref[side, pl.ds(i // per * ROWS, ROWS), :]
            turn = (-(i % per) * edge) % LANES
            if turn:
                beside = pltpu.roll(beside, turn, 1)
            beside = jnp.where(lane < edge, beside, 0.0)
            if sines[j] > 0:
                along = jnp.where(lane == 0, 0.0, pltpu.roll(here, 1, 1))
            else:
                along = jnp.where(lane == LANES - 1, 0.0, pltpu.roll(here, LANES - 1, 1))
            moved = (
                here
                - speed * float(abs(cosines[j])) * (here - beside)
                - speed * float(abs(sines[j])) * (here - along)
            ) * half
            e_ref[j, pl.ds(PAD + kb * ROWS, ROWS), :] = moved
            total = total + moved
            drive = wind_ref[0:1, :] * float(cosines[j]) + wind_ref[1:2, :] * float(sines[j])
            w_ref[j, pl.ds(kb * ROWS, ROWS), :] = jnp.maximum(
                drive_rate * drive - GAIN / LIMITER * WIND_RATE, 0.0
            )
        acc_ref[pl.ds(kb * ROWS, ROWS), :] = total

    up_j, up_z = split(ANGLE_UP * dir_count / 360.0)
    down_j, down_z = split(ANGLE_DOWN * dir_count / 360.0)
    up_near, up_far = up_j + 1, up_j
    up_weight, up_rest = up_z, (1.0 - up_z) / up_z
    down_near, down_far = down_j, down_j + 1
    down_weight, down_rest = 1.0 - down_z, down_z / (1.0 - down_z)
    up_scale = GAIN_UP * GAIN * up_weight
    down_scale = GAIN_DOWN * GAIN * down_weight
    fold = (1.0 - UP_W) * up_weight
    up_tail = UP_W / (1.0 - UP_W)
    down_head = (1.0 - DOWN_W) * down_weight / fold
    down_tail = DOWN_W * down_weight / fold
    own = -2.0 / fold

    def stage_a(kb, carry):
        base = kb * ROWS
        strength = table_ref[1, pl.ds(base, ROWS), :]
        up, up_c, down, down_c, quads = {}, {}, {}, {}, {}

        def read(j, offset):
            return e_ref[j, pl.ds(base + PAD + offset, ROWS), :]

        def get_up(j):
            j %= dir_count
            if j not in up:
                up[j] = (up_scale * (1.0 - UP_W)) * read(j, UP_K) + (up_scale * UP_W) * read(j, UP_K + 1)
                up_c[j] = up[j] * up_rest
            return up[j], up_c[j]

        def get_down(j):
            j %= dir_count
            if j not in down:
                down[j] = (down_scale * (1.0 - DOWN_W)) * read(j, DOWN_K) + (
                    down_scale * DOWN_W
                ) * read(j, DOWN_K + 1)
                down_c[j] = down[j] * down_rest
            return down[j], down_c[j]

        def get_quads(j):
            j %= dir_count
            if j not in quads:
                here = read(j, 0)
                gain = here * strength
                pair = []
                for sign in (1, -1):
                    plus = get_up(j + sign * up_near)[0] + get_up(j + sign * up_far)[1]
                    minus = get_down(j + sign * down_near)[0] + get_down(j + sign * down_far)[1]
                    pair.append(gain * (here * (plus + minus) - plus * minus))
                quads[j] = pair
            return quads[j]

        for j in range(dir_count):
            u_ref[j, pl.ds(base + PAD, ROWS), :] = (
                get_quads(j - up_near)[0] + get_quads(j + up_near)[1]
            ) + up_rest * (get_quads(j - up_far)[0] + get_quads(j + up_far)[1])
            d_ref[j, pl.ds(base + PAD, ROWS), :] = (
                get_quads(j - down_near)[0] + get_quads(j + down_near)[1]
            ) + down_rest * (get_quads(j - down_far)[0] + get_quads(j + down_far)[1])
            n_ref[j, pl.ds(base, ROWS), :] = own * (get_quads(j)[0] + get_quads(j)[1])
        return carry

    def stage_b(kb, carry):
        base = kb * ROWS
        decay = c_ref[pl.ds(base, ROWS), :]
        total = jnp.zeros((ROWS, LANES), jnp.float32)
        for j in range(dir_count):
            here = e_ref[j, pl.ds(base + PAD, ROWS), :]
            rate = here * (w_ref[j, pl.ds(base, ROWS), :] - decay) + n_ref[j, pl.ds(base, ROWS), :]
            rate = rate + (
                u_ref[j, pl.ds(base + PAD - UP_K, ROWS), :]
                + up_tail * u_ref[j, pl.ds(base + PAD - UP_K - 1, ROWS), :]
            )
            rate = rate + (
                down_head * d_ref[j, pl.ds(base + PAD - DOWN_K, ROWS), :]
                + down_tail * d_ref[j, pl.ds(base + PAD - DOWN_K - 1, ROWS), :]
            )
            here = here + (LIMITER / SUB / GAIN) * jnp.tanh(rate)
            e_ref[j, pl.ds(base + PAD, ROWS), :] = here
            total = total + here
        acc_ref[pl.ds(base, ROWS), :] = total
        return carry

    def sub_step(index, carry):
        steepness = jnp.sum(acc_ref[...] * table_ref[3], axis=0, keepdims=True)
        c_ref[...] = steepness * table_ref[4]
        lax.fori_loop(0, blocks, stage_a, 0)
        lax.fori_loop(0, blocks, stage_b, 0)
        return carry

    lax.fori_loop(0, SUB, sub_step, 0)

    full = mask * GAIN

    def result(j, kb):
        return e_ref[j, pl.ds(PAD + kb * ROWS, ROWS), :] * full

    for kb in range(blocks):
        for j in range(dir_count):
            if last:
                out_ref[pl.ds(kb * ROWS * dir_count + j, ROWS, stride=dir_count), :] = result(j, kb)
            else:
                out_ref[j, pl.ds(kb * ROWS, ROWS), :] = result(j, kb)
    if last:
        energy = jnp.sum(acc_ref[...], axis=0, keepdims=True) * (full * (1.0 / (freq_count * dir_count)))
        slots = energy_ref.shape[1]
        chosen = (
            deal_ref[...] == lax.broadcasted_iota(jnp.int32, (LANES, slots), 1)
        ).astype(jnp.float32)
        energy_ref[...] = jnp.dot(
            jnp.broadcast_to(energy, (ROWS, LANES)), chosen,
            precision=lax.Precision.HIGHEST, preferred_element_type=jnp.float32,
        )[0:1]
    else:
        store_packs(result, pair_out, next_out, parity, freq_count, dir_count, edge, lane)


def coast_width(tile_count, cell_count):
    capacity = cell_count // tile_count
    spread = tile_count * (tile_count - 8) // 8
    most = -(-spread // (tile_count - 1)) * capacity
    width = ROWS
    while width < most:
        width *= 2
    return min(width, LANES)


def shards(spectrum, sea_mask, card_deal, wind):
    freq_count, dir_count, row_count, row_width = spectrum.shape
    cell_count = row_count * row_width
    tile_count = lax.axis_size("tile")
    slot_count = cell_count // 8
    edge = coast_width(tile_count, cell_count)
    here = lax.axis_index("tile")
    parity = (here % 2).astype(jnp.int32).reshape(1)
    flat = spectrum.reshape(freq_count * dir_count, cell_count)
    mask = sea_mask.reshape(1, cell_count)
    winds = wind.reshape(2, cell_count)
    deal = card_deal.reshape(cell_count, 1)
    table = jnp.asarray(tables(freq_count, dir_count))
    rows = pack_rows(dir_count, freq_count, edge)
    packed = jax.ShapeDtypeStruct((rows, LANES), jnp.float32)
    smem = pl.BlockSpec(memory_space=pltpu.SMEM)
    vmem = pl.BlockSpec(memory_space=pltpu.VMEM)
    params = pltpu.CompilerParams(vmem_limit_bytes=48 * 1024 * 1024)
    padded = pltpu.VMEM((dir_count, freq_count + 2 * PAD, LANES), jnp.float32)
    plain = pltpu.VMEM((dir_count, freq_count, LANES), jnp.float32)
    column = pltpu.VMEM((freq_count, LANES), jnp.float32)
    scratch = [padded, padded, padded, plain, plain, column, column, pltpu.VMEM((2, rows, LANES), jnp.float32)]

    def exchange(pair_out, next_out):
        next_in = lax.ppermute(
            next_out, "tile",
            [(i, i + 1 if i % 2 else i - 1) for i in range(1, tile_count - 1)],
        )
        pair_in = lax.ppermute(pair_out, "tile", [(i, i ^ 1) for i in range(tile_count)])
        return pair_in, next_in

    pair_in, next_in = exchange(*pl.pallas_call(
        functools.partial(edges_kernel, freq_count, dir_count, edge),
        out_shape=(packed, packed),
        in_specs=[smem, vmem, vmem],
        out_specs=(vmem, vmem),
        compiler_params=params,
        name="edges",
    )(parity, flat, mask))
    field, pair_out, next_out = pl.pallas_call(
        functools.partial(step_kernel, freq_count, dir_count, edge, True, False),
        out_shape=(jax.ShapeDtypeStruct((dir_count, freq_count, LANES), jnp.float32), packed, packed),
        in_specs=[smem] + [vmem] * 6,
        out_specs=(vmem,) * 3,
        scratch_shapes=scratch,
        compiler_params=params,
        name="first_step",
    )(parity, flat, mask, winds, table, pair_in, next_in)
    pair_in, next_in = exchange(pair_out, next_out)
    out, energy = pl.pallas_call(
        functools.partial(step_kernel, freq_count, dir_count, edge, False, True),
        out_shape=(
            jax.ShapeDtypeStruct((freq_count * dir_count, LANES), jnp.float32),
            jax.ShapeDtypeStruct((1, tile_count * slot_count), jnp.float32),
        ),
        in_specs=[smem] + [vmem] * 7,
        out_specs=(vmem,) * 2,
        scratch_shapes=scratch,
        compiler_params=params,
        name="second_step",
    )(parity, field, mask, winds, table, pair_in, next_in, deal)
    shared = lax.all_to_all(
        energy.reshape(tile_count, slot_count), "tile", split_axis=0, concat_axis=0, tiled=True
    )
    card_energy = jnp.sum(shared, axis=0)
    return out.reshape(freq_count, dir_count, row_count, row_width), card_energy


def solution(mesh):
    placed = (
        P(None, None, ("groups", "tile"), None),
        P(("groups", "tile"), None),
        P(("groups", "tile"), None),
        P(None, ("groups", "tile"), None),
    )
    return jax.shard_map(
        shards,
        mesh=mesh,
        in_specs=placed,
        out_specs=(P(None, None, ("groups", "tile"), None), P(("groups", "tile"))),
        check_vma=False,
    )
```

profile of v0, /device:TPU:0, one launch (start us, length us, event | category | flops | bytes accessed | tf_op | source)
XLA Modules:
  0.0 53.3 jit_solution(9681579364643363335)
XLA Ops:
  0.6 0.0 copy-start.2
  0.6 0.6 %copy-done.2 = s32[1,128]{1,0:T(1,128)S(1)} copy-done((s32[1,128]{1,0:T(1,128)S(1)}, s32[1,128]{1,0:T(1,128)}, u32[]{:S(2)}) %copy-start.2) | copy-done | bytes 536
  1.3 0.0 copy-start
  1.3 1.1 %copy-done = f32[40,36,1,128]{3,2,1,0:T(1,128)S(1)} copy-done((f32[40,36,1,128]{3,2,1,0:T(1,128)S(1)}, f32[40,36,1,128]{3,2,1,0:T(1,128)}, u32[]{:S(2)}) %copy-start) | copy-done | bytes 737304
  2.4 0.0 copy-start.1
  2.4 0.3 edges.1
  2.7 0.5 collective-permute-start
  3.2 0.0 copy-start.3
  3.2 0.8 %collective-permute-start.1 = (f32[96,128]{1,0:T(8,128)S(1)}, f32[96,128]{1,0:T(8,128)S(1)}, u32[]{:S(2)}, u32[]{:S(2)}) collective-permute-start(f32[96,128]{1,0:T(8,128)S(1)} %get-tuple-element.10), channel_id=1, source_target_pairs={{1,2},{2,1},{3,4},{4,3},{5,6},{6,5},{7,8},{8,7},{9,10},{10,9},{11,... | collective-permute-start | bytes 147464 | tf_op jit(solution)/shard_map/ppermute | solution.py:339
  4.0 0.1 collective-permute-done.pair_ref
  4.1 0.0 collective-permute-done.1.next_ref
  4.1 0.0 copy-done.1
  4.1 0.0 copy-done.3
  4.1 11.1 %first_step.1 = (f32[36,40,128]{2,1,0:T(8,128)S(1)}, f32[96,128]{1,0:T(8,128)S(1)}, f32[96,128]{1,0:T(8,128)S(1)}) custom-call(s32[1]{0:T(128)} %bitcast.parity_ref, f32[1440,128]{1,0:T(8,128)S(1)} %bitcast.7, s32[1,128]{1,0:T(1,128)S(1)} %copy-done.2, f32[2,128]{1,0:T(2,128)S(1)} %bitcast.8, f32[5,40,128]{2,1,0:T(8,128)S(1)} %copy-done.1, ...), custom_call_target="tpu_custom_call" | custom-call | tf_op jit(solution)/shard_map/first_step/pallas_call | solution.py:354
  15.2 5.5 %collective-permute-start.2 = (f32[96,128]{1,0:T(8,128)S(1)}, f32[96,128]{1,0:T(8,128)S(1)}, u32[]{:S(2)}, u32[]{:S(2)}) collective-permute-start(f32[96,128]{1,0:T(8,128)S(1)} %get-tuple-element.12), channel_id=1, source_target_pairs={{0,1},{1,0},{2,3},{3,2},{4,5},{5,4},{6,7},{7,6},{8,9},{9,8},{10,11... | collective-permute-start | bytes 147464 | tf_op jit(solution)/shard_map/ppermute | solution.py:343
  20.8 0.0 copy-start.4
  20.8 0.8 %collective-permute-start.3 = (f32[96,128]{1,0:T(8,128)S(1)}, f32[96,128]{1,0:T(8,128)S(1)}, u32[]{:S(2)}, u32[]{:S(2)}) collective-permute-start(f32[96,128]{1,0:T(8,128)S(1)} %get-tuple-element.13), channel_id=1, source_target_pairs={{1,2},{2,1},{3,4},{4,3},{5,6},{6,5},{7,8},{8,7},{9,10},{10,9},{11,... | collective-permute-start | bytes 147464 | tf_op jit(solution)/shard_map/ppermute | solution.py:339
  21.5 0.0 copy-done.4
  21.6 0.1 copy.11.rest_0_
  21.7 0.0 collective-permute-done.2.pair_ref
  21.7 0.0 collective-permute-done.3.next_ref
  21.7 11.8 %second_step.1 = (f32[1440,128]{1,0:T(8,128)}, f32[1,256]{1,0:T(1,128)S(1)}) custom-call(s32[1]{0:T(128)} %bitcast.parity_ref, f32[36,40,128]{2,1,0:T(8,128)S(1)} %get-tuple-element.11.in_ref, s32[1,128]{1,0:T(1,128)S(1)} %copy-done.2, f32[2,128]{1,0:T(2,128)S(1)} %bitcast.9, f32[5,40,128]{2,1,0:T(8,128)S(1)} %copy-done.1, ...), custom_call_target="tpu_custom_call" | custom-call | tf_op jit(solution)/shard_map/second_step/pallas_call | solution.py:364
  33.5 0.5 broadcast.4
  34.0 0.7 %reduce.4 = f32[256]{0:T(256)S(1)} reduce(f32[1,256]{1,0:T(1,128)S(1)} %get-tuple-element.15, f32[]{:T(128)} %broadcast.4), dimensions={0}, to_apply=%get-tuple-element.15.reduce_sub_computation.3 | reduce | bytes 2052 | tf_op jit(solution)/shard_map/second_step/pallas_call | solution.py:364
  34.7 0.1 all_to_all.6
  34.8 18.0 %all_to_all.9 = f32[16,1,16]{2,1,0:T(1,128)S(1)} all-to-all(f32[16,1,16]{2,1,0:T(1,128)S(1)} %bitcast.10), channel_id=1, replica_groups=mesh['groups'=2,'tile'=16] {'tile'}, dimensions={0} | all-to-all | bytes 2048 | tf_op jit(solution)/shard_map/all_to_all | solution.py:376
  52.8 0.5 %reduce_sum.9 = f32[16]{0:T(128)} reduce(f32[16,1,16]{2,1,0:T(1,128)S(1)} %all_to_all.9, f32[]{:T(128)} %constant.20.clone.1), dimensions={0,1}, to_apply=%region_0.1 | reduce | flops 240 | bytes 1092 | tf_op jit(solution)/shard_map/reduce_sum | solution.py:379
Async XLA Ops:
  0.6 0.7 %copy-start.2 = (s32[1,128]{1,0:T(1,128)S(1)}, s32[1,128]{1,0:T(1,128)}, u32[]{:S(2)}) copy-start(s32[1,128]{1,0:T(1,128)} %mask_ref.5) | copy-start | bytes 1540
  1.3 1.1 %copy-start = (f32[40,36,1,128]{3,2,1,0:T(1,128)S(1)}, f32[40,36,1,128]{3,2,1,0:T(1,128)}, u32[]{:S(2)}) copy-start(f32[40,36,1,128]{3,2,1,0:T(1,128)} %param.5) | copy-start | bytes 2211844
  2.4 1.7 %copy-start.1 = (f32[5,40,128]{2,1,0:T(8,128)S(1)}, f32[5,40,128]{2,1,0:T(8,128)}, u32[]{:S(2)}) copy-start(f32[5,40,128]{2,1,0:T(8,128)} %constant.21.clone.table_ref) | copy-start | bytes 307204
  2.7 1.4 %collective-permute-start = (f32[96,128]{1,0:T(8,128)S(1)}, f32[96,128]{1,0:T(8,128)S(1)}, u32[]{:S(2)}, u32[]{:S(2)}) collective-permute-start(f32[96,128]{1,0:T(8,128)S(1)} %get-tuple-element.9), channel_id=1, source_target_pairs={{0,1},{1,0},{2,3},{3,2},{4,5},{5,4},{6,7},{7,6},{8,9},{9,8},{10,11... | collective-permute-start | bytes 147464 | tf_op jit(solution)/shard_map/ppermute | solution.py:343
  3.2 0.9 %copy-start.3 = (f32[2,1,128]{2,1,0:T(1,128)S(1)}, f32[2,1,128]{2,1,0:T(1,128)}, u32[]{:S(2)}) copy-start(f32[2,1,128]{2,1,0:T(1,128)} %param.8) | copy-start | bytes 3076
  3.2 0.9 %collective-permute-start.1 = (f32[96,128]{1,0:T(8,128)S(1)}, f32[96,128]{1,0:T(8,128)S(1)}, u32[]{:S(2)}, u32[]{:S(2)}) collective-permute-start(f32[96,128]{1,0:T(8,128)S(1)} %get-tuple-element.10), channel_id=1, source_target_pairs={{1,2},{2,1},{3,4},{4,3},{5,6},{6,5},{7,8},{8,7},{9,10},{10,9},{11,... | collective-permute-start | bytes 147464 | tf_op jit(solution)/shard_map/ppermute | solution.py:339
  15.2 6.4 %collective-permute-start.2 = (f32[96,128]{1,0:T(8,128)S(1)}, f32[96,128]{1,0:T(8,128)S(1)}, u32[]{:S(2)}, u32[]{:S(2)}) collective-permute-start(f32[96,128]{1,0:T(8,128)S(1)} %get-tuple-element.12), channel_id=1, source_target_pairs={{0,1},{1,0},{2,3},{3,2},{4,5},{5,4},{6,7},{7,6},{8,9},{9,8},{10,11... | collective-permute-start | bytes 147464 | tf_op jit(solution)/shard_map/ppermute | solution.py:343
  20.8 0.8 %copy-start.4 = (s32[1,128]{1,0:T(1,128)S(1)}, s32[1,128]{1,0:T(1,128)}, u32[]{:S(2)}) copy-start(s32[1,128]{1,0:T(1,128)} %param.7) | copy-start | bytes 1540
  20.8 0.9 %collective-permute-start.3 = (f32[96,128]{1,0:T(8,128)S(1)}, f32[96,128]{1,0:T(8,128)S(1)}, u32[]{:S(2)}, u32[]{:S(2)}) collective-permute-start(f32[96,128]{1,0:T(8,128)S(1)} %get-tuple-element.13), channel_id=1, source_target_pairs={{1,2},{2,1},{3,4},{4,3},{5,6},{6,5},{7,8},{8,7},{9,10},{10,9},{11,... | collective-permute-start | bytes 147464 | tf_op jit(solution)/shard_map/ppermute | solution.py:339
where the time goes:
time: 53.6 us; the launch traced here: 53.3 us
  Pallas kernels  23.2 us (43%)
  blocking collectives  18 us (34%)
  starting transfers between devices  7.6 us (14%)
  local copies, waits for them, and re-layouts  2.48 us (5%)
  other arithmetic  1.21 us (2%)
  between operations  0.71 us (1%)
    pallas_call x2, Pallas kernels, shards(): pl.pallas_call(functools.partial(step_kernel, freq_count, dir_count, edge...  22.9 us
    all_to_all x1, blocking collectives, shards(): lax.all_to_all(energy.reshape(tile_count, slot_count), 'tile', split_axis...  18 us
    ppermute x2, starting transfers between devices, exchange(): lax.ppermute(pair_out, 'tile', [(i, i ^ 1) for i in range(tile_count)])  6.03 us
    unnamed x10, local copies, waits for them, and re-layouts  1.77 us
    ppermute x2, starting transfers between devices, exchange(): lax.ppermute(next_out, 'tile', [(i, i + 1 if i % 2 else i - 1) for i in r...  1.57 us
  transfers between devices with their start and end apart: 4, of which 1 were waited for; matrix products, arithmetic and copies ran while one was open for 0% of the time, Pallas kernels for 0%

commit v1 on v0

--- a/solution.py
+++ b/solution.py
@@ -116,7 +116,7 @@
 
 
 def step_kernel(
-    freq_count, dir_count, edge, first, last,
+    freq_count, dir_count, edge, slot_count, first, last,
     parity_ref, in_ref, mask_ref, wind_ref, table_ref, pair_ref, next_ref, *rest
 ):
     if last:
@@ -139,15 +139,17 @@
             ref[j, pl.ds(0, PAD), :] = zero
             ref[j, pl.ds(PAD + freq_count, PAD), :] = zero
 
+    inner = (parity_ref[1] == 0).astype(jnp.float32)
+
     @pl.when(parity == 0)
     def _():
-        back_ref[0] = next_ref[...]
+        back_ref[0] = next_ref[...] * inner
         back_ref[1] = pair_ref[...]
 
     @pl.when(parity == 1)
     def _():
         back_ref[0] = pair_ref[...]
-        back_ref[1] = next_ref[...]
+        back_ref[1] = next_ref[...] * inner
 
     place = {}
     for forward in (True, False):
@@ -290,14 +292,16 @@
                 out_ref[j, pl.ds(kb * ROWS, ROWS), :] = result(j, kb)
     if last:
         energy = jnp.sum(acc_ref[...], axis=0, keepdims=True) * (full * (1.0 / (freq_count * dir_count)))
-        slots = energy_ref.shape[1]
-        chosen = (
-            deal_ref[...] == lax.broadcasted_iota(jnp.int32, (LANES, slots), 1)
-        ).astype(jnp.float32)
-        energy_ref[...] = jnp.dot(
-            jnp.broadcast_to(energy, (ROWS, LANES)), chosen,
+        deal = deal_ref[...]
+        cards = energy_ref.shape[0]
+        card = lax.broadcasted_iota(jnp.int32, (cards, LANES), 0) * slot_count
+        slot = lax.broadcasted_iota(jnp.int32, (LANES, LANES), 0)
+        to_card = jnp.where((deal >= card) & (deal < card + slot_count), energy, 0.0)
+        to_slot = (lax.rem(jnp.maximum(deal, 0), slot_count) == slot).astype(jnp.float32)
+        energy_ref[...] = lax.dot_general(
+            to_card, to_slot, (((1,), (1,)), ((), ())),
             precision=lax.Precision.HIGHEST, preferred_element_type=jnp.float32,
-        )[0:1]
+        )
     else:
         store_packs(result, pair_out, next_out, parity, freq_count, dir_count, edge, lane)
 
@@ -319,11 +323,12 @@
     slot_count = cell_count // 8
     edge = coast_width(tile_count, cell_count)
     here = lax.axis_index("tile")
-    parity = (here % 2).astype(jnp.int32).reshape(1)
+    at_end = (here == 0) | (here == tile_count - 1)
+    parity = jnp.stack([here % 2, at_end.astype(jnp.int32)])
     flat = spectrum.reshape(freq_count * dir_count, cell_count)
     mask = sea_mask.reshape(1, cell_count)
     winds = wind.reshape(2, cell_count)
-    deal = card_deal.reshape(cell_count, 1)
+    deal = card_deal.reshape(1, cell_count)
     table = jnp.asarray(tables(freq_count, dir_count))
     rows = pack_rows(dir_count, freq_count, edge)
     packed = jax.ShapeDtypeStruct((rows, LANES), jnp.float32)
@@ -335,11 +340,17 @@
     column = pltpu.VMEM((freq_count, LANES), jnp.float32)
     scratch = [padded, padded, padded, plain, plain, column, column, pltpu.VMEM((2, rows, LANES), jnp.float32)]
 
+    group_count = lax.axis_size("groups")
+    chip_swap = []
+    for g in range(group_count):
+        for i in range(tile_count):
+            other, there = g, (i + 1 if i % 2 else i - 1)
+            if not 0 <= there < tile_count:
+                other, there = (g ^ 1 if g ^ 1 < group_count else g), i
+            chip_swap.append((g * tile_count + i, other * tile_count + there))
+
     def exchange(pair_out, next_out):
-        next_in = lax.ppermute(
-            next_out, "tile",
-            [(i, i + 1 if i % 2 else i - 1) for i in range(1, tile_count - 1)],
-        )
+        next_in = lax.ppermute(next_out, ("groups", "tile"), chip_swap)
         pair_in = lax.ppermute(pair_out, "tile", [(i, i ^ 1) for i in range(tile_count)])
         return pair_in, next_in
 
@@ -352,7 +363,7 @@
         name="edges",
     )(parity, flat, mask))
     field, pair_out, next_out = pl.pallas_call(
-        functools.partial(step_kernel, freq_count, dir_count, edge, True, False),
+        functools.partial(step_kernel, freq_count, dir_count, edge, slot_count, True, False),
         out_shape=(jax.ShapeDtypeStruct((dir_count, freq_count, LANES), jnp.float32), packed, packed),
         in_specs=[smem] + [vmem] * 6,
         out_specs=(vmem,) * 3,
@@ -362,10 +373,10 @@
     )(parity, flat, mask, winds, table, pair_in, next_in)
     pair_in, next_in = exchange(pair_out, next_out)
     out, energy = pl.pallas_call(
-        functools.partial(step_kernel, freq_count, dir_count, edge, False, True),
+        functools.partial(step_kernel, freq_count, dir_count, edge, slot_count, False, True),
         out_shape=(
             jax.ShapeDtypeStruct((freq_count * dir_count, LANES), jnp.float32),
-            jax.ShapeDtypeStruct((1, tile_count * slot_count), jnp.float32),
+            jax.ShapeDtypeStruct((tile_count, LANES), jnp.float32),
         ),
         in_specs=[smem] + [vmem] * 7,
         out_specs=(vmem,) * 2,
@@ -374,9 +385,9 @@
         name="second_step",
     )(parity, field, mask, winds, table, pair_in, next_in, deal)
     shared = lax.all_to_all(
-        energy.reshape(tile_count, slot_count), "tile", split_axis=0, concat_axis=0, tiled=True
+        energy.reshape(tile_count, 1, LANES), "tile", split_axis=0, concat_axis=0, tiled=True
     )
-    card_energy = jnp.sum(shared, axis=0)
+    card_energy = jnp.sum(shared, axis=(0, 1))[:slot_count]
     return out.reshape(freq_count, dir_count, row_count, row_width), card_energy
 
 

time: 53.6 us -> 50.1 us (0.935)
  blocking collectives: 18 us -> 12.5 us
  waiting for transfers between devices: 0.1 us -> 4.14 us
  starting transfers between devices: 7.6 us -> 5.29 us
  Pallas kernels: 23.2 us -> 24.8 us
  local copies, waits for them, and re-layouts: 2.48 us -> 1.78 us
  other arithmetic: 1.21 us -> 0.62 us
    all_to_all x1, blocking collectives: 18 us -> 12.5 us  [shards(): lax.all_to_all(energy.reshape(tile_count, 1, LANES), 'tile', split_axis=0...]
    ppermute x2, starting transfers between devices: 6.03 us -> 0.7 us  [exchange(): lax.ppermute(pair_out, 'tile', [(i, i ^ 1) for i in range(tile_count)])]
    ppermute x2, waiting for transfers between devices: 0.01 us -> 4.13 us  [exchange(): next_in = lax.ppermute(next_out, ('groups', 'tile'), chip_swap)]
    ppermute x2, starting transfers between devices: 1.57 us -> 4.59 us  [exchange(): next_in = lax.ppermute(next_out, ('groups', 'tile'), chip_swap)]
    pallas_call x2, Pallas kernels: 22.9 us -> 24 us  [shards(): pl.pallas_call(functools.partial(step_kernel, freq_count, dir_count, edge...]
    pallas_call x1 -> x0, other arithmetic: 0.66 us -> none  [shards(): pl.pallas_call(functools.partial(step_kernel, freq_count, dir_count, edge...]
    pallas_call x1, Pallas kernels: 0.3 us -> 0.84 us  [shards(): pl.pallas_call(functools.partial(edges_kernel, freq_count, dir_count, edg...]
  transfers between devices with their start and end apart: 4 -> 4, of which waited for: 1 -> 2; matrix products, arithmetic and copies ran while one was open for 0% -> 0% of each run, Pallas kernels for 0% -> 0%
where the time goes in v1:
time: 50.1 us; the launch traced here: 49.9 us
  Pallas kernels  24.8 us (50%)
  blocking collectives  12.5 us (25%)
  starting transfers between devices  5.29 us (11%)
  waiting for transfers between devices  4.14 us (8%)
  local copies, waits for them, and re-layouts  1.78 us (4%)
  between operations  0.67 us (1%)
  other arithmetic  0.62 us (1%)
    pallas_call x2, Pallas kernels, shards(): pl.pallas_call(functools.partial(step_kernel, freq_count, dir_count, edge...  24 us
    all_to_all x1, blocking collectives, shards(): lax.all_to_all(energy.reshape(tile_count, 1, LANES), 'tile', split_axis=0...  12.5 us
    ppermute x2, starting transfers between devices, exchange(): next_in = lax.ppermute(next_out, ('groups', 'tile'), chip_swap)  4.59 us
    ppermute x2, waiting for transfers between devices, exchange(): next_in = lax.ppermute(next_out, ('groups', 'tile'), chip_swap)  4.13 us
    unnamed x10, local copies, waits for them, and re-layouts  1.78 us
  transfers between devices with their start and end apart: 4, of which 2 were waited for; matrix products, arithmetic and copies ran while one was open for 0% of the time, Pallas kernels for 0%

profile of v1, /device:TPU:0, one launch (start us, length us, event | category | flops | bytes accessed | tf_op | source)
XLA Modules:
  0.0 49.9 jit_solution(12310298136712484960)
XLA Ops:
  0.6 0.1 pad_add_fusion.parity_ref
  0.7 0.0 copy-start.2
  0.7 0.7 %copy-done.2 = s32[1,128]{1,0:T(1,128)S(1)} copy-done((s32[1,128]{1,0:T(1,128)S(1)}, s32[1,128]{1,0:T(1,128)}, u32[]{:S(2)}) %copy-start.2) | copy-done | bytes 536
  1.4 0.0 copy-start
  1.4 1.1 %copy-done = f32[40,36,1,128]{3,2,1,0:T(1,128)S(1)} copy-done((f32[40,36,1,128]{3,2,1,0:T(1,128)S(1)}, f32[40,36,1,128]{3,2,1,0:T(1,128)}, u32[]{:S(2)}) %copy-start) | copy-done | bytes 737304
  2.5 0.0 copy-start.1
  2.5 0.8 %edges.1 = (f32[96,128]{1,0:T(8,128)S(1)}, f32[96,128]{1,0:T(8,128)S(1)}) custom-call(s32[2]{0:T(128)S(1)} %pad_add_fusion.parity_ref, f32[1440,128]{1,0:T(8,128)S(1)} %bitcast.9, s32[1,128]{1,0:T(1,128)S(1)} %copy-done.2), custom_call_target="tpu_custom_call" | custom-call | tf_op jit(solution)/shard_map/edges/pallas_call | solution.py:357
  3.3 0.5 %collective-permute-start = (f32[96,128]{1,0:T(8,128)S(1)}, f32[96,128]{1,0:T(8,128)S(1)}, u32[]{:S(2)}, u32[]{:S(2)}) collective-permute-start(f32[96,128]{1,0:T(8,128)S(1)} %get-tuple-element.9), channel_id=1, source_target_pairs={{0,1},{1,0},{2,3},{3,2},{4,5},{5,4},{6,7},{7,6},{8,9},{9,8},{10,11... | collective-permute-start | bytes 147464 | tf_op jit(solution)/shard_map/ppermute | solution.py:354
  3.9 0.0 copy-start.3
  3.9 2.6 %collective-permute-start.1 = (f32[96,128]{1,0:T(8,128)S(1)}, f32[96,128]{1,0:T(8,128)S(1)}, u32[]{:S(2)}, u32[]{:S(2)}) collective-permute-start(f32[96,128]{1,0:T(8,128)S(1)} %get-tuple-element.10), channel_id=1, source_target_pairs={{0,16},{1,2},{2,1},{3,4},{4,3},{5,6},{6,5},{7,8},{8,7},{9,10},{10,... | collective-permute-start | bytes 147464 | tf_op jit(solution)/shard_map/ppermute | solution.py:353
  6.4 0.0 collective-permute-done.pair_ref
  6.4 2.1 %collective-permute-done.1.next_ref = f32[96,128]{1,0:T(8,128)S(1)} collective-permute-done((f32[96,128]{1,0:T(8,128)S(1)}, f32[96,128]{1,0:T(8,128)S(1)}, u32[]{:S(2)}, u32[]{:S(2)}) %collective-permute-start.1) | collective-permute-done | bytes 49184 | tf_op jit(solution)/shard_map/ppermute | solution.py:353
  8.5 0.0 copy-done.1
  8.5 0.0 copy-done.3
  8.5 11.6 %first_step.1 = (f32[36,40,128]{2,1,0:T(8,128)S(1)}, f32[96,128]{1,0:T(8,128)S(1)}, f32[96,128]{1,0:T(8,128)S(1)}) custom-call(s32[2]{0:T(128)S(1)} %pad_add_fusion.parity_ref, f32[1440,128]{1,0:T(8,128)S(1)} %bitcast.10, s32[1,128]{1,0:T(1,128)S(1)} %copy-done.2, f32[2,128]{1,0:T(2,128)S(1)} %bitcast.12, f32[5,40,128]{2,1,0:T(8,128)S(1)} %copy-done.1, ...), custom_call_target="tpu_custom_call" | custom-call | tf_op jit(solution)/shard_map/first_step/pallas_call | solution.py:365
  20.2 0.2 collective-permute-start.2
  20.3 0.0 copy-start.4
  20.3 2.0 %collective-permute-start.3 = (f32[96,128]{1,0:T(8,128)S(1)}, f32[96,128]{1,0:T(8,128)S(1)}, u32[]{:S(2)}, u32[]{:S(2)}) collective-permute-start(f32[96,128]{1,0:T(8,128)S(1)} %get-tuple-element.13), channel_id=1, source_target_pairs={{0,16},{1,2},{2,1},{3,4},{4,3},{5,6},{6,5},{7,8},{8,7},{9,10},{10,... | collective-permute-start | bytes 147464 | tf_op jit(solution)/shard_map/ppermute | solution.py:353
  22.4 0.0 collective-permute-done.2.pair_ref
  22.4 2.1 %collective-permute-done.3.next_ref = f32[96,128]{1,0:T(8,128)S(1)} collective-permute-done((f32[96,128]{1,0:T(8,128)S(1)}, f32[96,128]{1,0:T(8,128)S(1)}, u32[]{:S(2)}, u32[]{:S(2)}) %collective-permute-start.3) | collective-permute-done | bytes 49184 | tf_op jit(solution)/shard_map/ppermute | solution.py:353
  24.4 0.0 copy-done.4
  24.4 12.4 %second_step.1 = (f32[1440,128]{1,0:T(8,128)}, f32[16,128]{1,0:T(8,128)S(1)}) custom-call(s32[2]{0:T(128)S(1)} %pad_add_fusion.parity_ref, f32[36,40,128]{2,1,0:T(8,128)S(1)} %get-tuple-element.11.in_ref, s32[1,128]{1,0:T(1,128)S(1)} %copy-done.2, f32[2,128]{1,0:T(2,128)S(1)} %bitcast.13, f32[5,40,128]{2,1,0:T(8,128)S(1)} %copy-done.1, ...), custom_call_target="tpu_custom_call" | custom-call | tf_op jit(solution)/shard_map/second_step/pallas_call | solution.py:375
  36.8 12.5 %all_to_all.5 = f32[16,1,128]{2,1,0:T(1,128)S(1)} all-to-all(f32[16,1,128]{2,1,0:T(1,128)S(1)} %bitcast.11), channel_id=1, replica_groups=mesh['groups'=2,'tile'=16] {'tile'}, dimensions={0} | all-to-all | bytes 16384 | tf_op jit(solution)/shard_map/all_to_all | solution.py:387
  49.3 0.5 %reduce_sum.9 = f32[128]{0:T(128)} reduce(f32[16,1,128]{2,1,0:T(1,128)S(1)} %all_to_all.5, f32[]{:T(128)} %constant.23.clone.1), dimensions={0,1}, to_apply=%region_0.1 | reduce | flops 1920 | bytes 8708 | tf_op jit(solution)/shard_map/reduce_sum | solution.py:390
Async XLA Ops:
  0.7 0.7 %copy-start.2 = (s32[1,128]{1,0:T(1,128)S(1)}, s32[1,128]{1,0:T(1,128)}, u32[]{:S(2)}) copy-start(s32[1,128]{1,0:T(1,128)} %mask_ref.5) | copy-start | bytes 1540
  1.4 1.1 %copy-start = (f32[40,36,1,128]{3,2,1,0:T(1,128)S(1)}, f32[40,36,1,128]{3,2,1,0:T(1,128)}, u32[]{:S(2)}) copy-start(f32[40,36,1,128]{3,2,1,0:T(1,128)} %param.5) | copy-start | bytes 2211844
  2.5 6.0 %copy-start.1 = (f32[5,40,128]{2,1,0:T(8,128)S(1)}, f32[5,40,128]{2,1,0:T(8,128)}, u32[]{:S(2)}) copy-start(f32[5,40,128]{2,1,0:T(8,128)} %constant.24.clone.table_ref) | copy-start | bytes 307204
  3.3 3.1 %collective-permute-start = (f32[96,128]{1,0:T(8,128)S(1)}, f32[96,128]{1,0:T(8,128)S(1)}, u32[]{:S(2)}, u32[]{:S(2)}) collective-permute-start(f32[96,128]{1,0:T(8,128)S(1)} %get-tuple-element.9), channel_id=1, source_target_pairs={{0,1},{1,0},{2,3},{3,2},{4,5},{5,4},{6,7},{7,6},{8,9},{9,8},{10,11... | collective-permute-start | bytes 147464 | tf_op jit(solution)/shard_map/ppermute | solution.py:354
  3.9 4.6 %copy-start.3 = (f32[2,1,128]{2,1,0:T(1,128)S(1)}, f32[2,1,128]{2,1,0:T(1,128)}, u32[]{:S(2)}) copy-start(f32[2,1,128]{2,1,0:T(1,128)} %param.8) | copy-start | bytes 3076
  3.9 4.6 %collective-permute-start.1 = (f32[96,128]{1,0:T(8,128)S(1)}, f32[96,128]{1,0:T(8,128)S(1)}, u32[]{:S(2)}, u32[]{:S(2)}) collective-permute-start(f32[96,128]{1,0:T(8,128)S(1)} %get-tuple-element.10), channel_id=1, source_target_pairs={{0,16},{1,2},{2,1},{3,4},{4,3},{5,6},{6,5},{7,8},{8,7},{9,10},{10,... | collective-permute-start | bytes 147464 | tf_op jit(solution)/shard_map/ppermute | solution.py:353
  20.2 2.2 %collective-permute-start.2 = (f32[96,128]{1,0:T(8,128)S(1)}, f32[96,128]{1,0:T(8,128)S(1)}, u32[]{:S(2)}, u32[]{:S(2)}) collective-permute-start(f32[96,128]{1,0:T(8,128)S(1)} %get-tuple-element.12), channel_id=1, source_target_pairs={{0,1},{1,0},{2,3},{3,2},{4,5},{5,4},{6,7},{7,6},{8,9},{9,8},{10,11... | collective-permute-start | bytes 147464 | tf_op jit(solution)/shard_map/ppermute | solution.py:354
  20.3 4.1 %copy-start.4 = (s32[1,128]{1,0:T(1,128)S(1)}, s32[1,128]{1,0:T(1,128)}, u32[]{:S(2)}) copy-start(s32[1,128]{1,0:T(1,128)} %rest_0_.1) | copy-start | bytes 1540
  20.3 4.1 %collective-permute-start.3 = (f32[96,128]{1,0:T(8,128)S(1)}, f32[96,128]{1,0:T(8,128)S(1)}, u32[]{:S(2)}, u32[]{:S(2)}) collective-permute-start(f32[96,128]{1,0:T(8,128)S(1)} %get-tuple-element.13), channel_id=1, source_target_pairs={{0,16},{1,2},{2,1},{3,4},{4,3},{5,6},{6,5},{7,8},{8,7},{9,10},{10,... | collective-permute-start | bytes 147464 | tf_op jit(solution)/shard_map/ppermute | solution.py:353

commit v2 on v1

v2 whole, which is shorter than its diff:
```python
import functools
import math

import jax
import jax.numpy as jnp
import numpy as np
from jax import lax
from jax.experimental import pallas as pl
from jax.experimental.pallas import tpu as pltpu
from jax.sharding import PartitionSpec as P

STEPS = 2
SUB = 8
COURANT_TOP = 0.7
WIND_RATE = 0.15
DECAY_RATE = 0.3
QUAD_RATE = 0.5
LIMITER = 0.25
ANGLE_UP = -11.48
ANGLE_DOWN = 33.56
SHIFT_UP = math.log(1.25) / math.log(1.1)
SHIFT_DOWN = math.log(0.75) / math.log(1.1)
GAIN_UP = 1.25 ** (-4)
GAIN_DOWN = 0.75 ** (-4)
GAIN_BOTH = 0.9375 ** (-4)

LANES = 128
ROWS = 8
PAD = 4


def split(offset):
    base = math.floor(offset)
    return base, offset - base


GAIN = 2.0 * GAIN_BOTH / (GAIN_UP * GAIN_DOWN)
UP_K, UP_W = split(SHIFT_UP)
DOWN_K, DOWN_W = split(SHIFT_DOWN)

COAST = 16
NEAR = 42
REST = 14
FAR = COAST + REST + NEAR


class Pack:
    def __init__(self, blocks, width, dir_count, offset):
        self.blocks, self.width, self.offset = blocks, width, offset
        self.slabs = dir_count // blocks
        self.dir_count = dir_count

    def direction(self, block, slab):
        return (block * self.slabs + slab + self.offset) % self.dir_count

    def find(self, j):
        return divmod((j - self.offset) % self.dir_count, self.slabs)

    def next_block(self, value, lane):
        last = (self.blocks - 1) * self.width
        ahead = turn(value, -self.width)
        if self.blocks * self.width == LANES:
            return ahead
        return jnp.where(lane < last, ahead, turn(value, last))

    def block_before(self, value, lane):
        last = (self.blocks - 1) * self.width
        behind = turn(value, self.width)
        if self.blocks * self.width == LANES:
            return behind
        return jnp.where(lane >= self.width, behind, turn(value, -last))

    def over_blocks(self, value, lane):
        if self.blocks == 4:
            value = value + turn(value, 2 * self.width)
            return value + turn(value, self.width)
        total = value
        for b in range(1, self.blocks):
            total = total + turn(value, -b * self.width)
        spread = total
        for b in range(1, self.blocks):
            spread = jnp.where(lane >= b * self.width, turn(total, b * self.width), spread)
        return spread

    def rows(self):
        angles = 2.0 * math.pi * np.arange(self.dir_count) / self.dir_count
        out = np.zeros((4, 16, LANES))
        for r in range(self.slabs):
            for b in range(self.blocks):
                at = slice(b * self.width, (b + 1) * self.width)
                angle = angles[self.direction(b, r)]
                out[:, r, at] = np.array(
                    [math.cos(angle), math.sin(angle), abs(math.cos(angle)), abs(math.sin(angle))]
                )[:, None]
        return out.astype(np.float32)


def turn(value, by):
    by %= LANES
    return pltpu.roll(value, by, 1) if by else value


def lanes():
    return lax.broadcasted_iota(jnp.int32, (ROWS, LANES), 1)


def within(lane, first, count):
    return (lane >= first) & (lane < first + count)


def sine_up(j, dir_count):
    return math.sin(2.0 * math.pi * j / dir_count) > 0


def tables(freq_count, dir_count):
    levels = 3.0 ** (np.arange(freq_count) / (freq_count - 1))
    speeds = COURANT_TOP * 1.1 ** (-np.arange(freq_count, dtype=np.float64))
    up_j, up_z = split(ANGLE_UP * dir_count / 360.0)
    rate = (1.0 - UP_W) * up_z / LIMITER
    rows = [
        speeds,
        rate * QUAD_RATE * GAIN * GAIN * levels,
        GAIN / LIMITER * WIND_RATE * 0.5 * levels,
        GAIN / (dir_count * np.sum(levels)) * levels,
        GAIN / LIMITER * DECAY_RATE * levels,
    ]
    return np.broadcast_to(
        np.stack(rows)[:, :, None], (len(rows), freq_count, LANES)
    ).astype(np.float32)


def clear(ref, slabs, freq_count):
    zero = jnp.zeros((PAD, LANES), jnp.float32)
    for r in range(slabs):
        ref[r, pl.ds(0, PAD), :] = zero
        ref[r, pl.ds(PAD + freq_count, PAD), :] = zero


def set_wind(pack, freq_count, table_ref, angle_ref, aux, w_ref):
    for r in range(pack.slabs):
        drive = aux[0:1] * angle_ref[0, r:r + 1, :] + aux[1:2] * angle_ref[1, r:r + 1, :]
        for kb in range(freq_count // ROWS):
            at = pl.ds(kb * ROWS, ROWS)
            w_ref[r, at, :] = jnp.maximum(table_ref[2, at, :] * drive - GAIN / LIMITER * WIND_RATE, 0.0)


def sub_steps(pack, freq_count, table_ref, e_ref, u_ref, d_ref, n_ref, w_ref, acc_ref, c_ref):
    slabs, blocks = pack.slabs, freq_count // ROWS
    lane = lanes()
    up_j, up_z = split(ANGLE_UP * pack.dir_count / 360.0)
    down_j, down_z = split(ANGLE_DOWN * pack.dir_count / 360.0)
    up_near, up_far = up_j + 1, up_j
    up_weight, up_rest = up_z, (1.0 - up_z) / up_z
    down_near, down_far = down_j, down_j + 1
    down_weight, down_rest = 1.0 - down_z, down_z / (1.0 - down_z)
    up_scale = GAIN_UP * GAIN * up_weight
    down_scale = GAIN_DOWN * GAIN * down_weight
    fold = (1.0 - UP_W) * up_weight
    up_tail = UP_W / (1.0 - UP_W)
    down_head = (1.0 - DOWN_W) * down_weight / fold
    down_tail = DOWN_W * down_weight / fold
    own = -2.0 / fold

    def around(known, make, r):
        if r not in known:
            if r < 0:
                known[r] = pack.block_before(around(known, make, r + slabs), lane)
            elif r >= slabs:
                known[r] = pack.next_block(around(known, make, r - slabs), lane)
            else:
                known[r] = make(r)
        return known[r]

    def stage_a(kb):
        base = kb * ROWS
        strength = table_ref[1, pl.ds(base, ROWS), :]
        up, down, more, less, up_c, down_c = {}, {}, {}, {}, {}, {}

        def read(r, offset):
            return e_ref[r, pl.ds(base + PAD + offset, ROWS), :]

        def make_up(r):
            return (up_scale * (1.0 - UP_W)) * read(r, UP_K) + (up_scale * UP_W) * read(r, UP_K + 1)

        def make_down(r):
            return (down_scale * (1.0 - DOWN_W)) * read(r, DOWN_K) + (down_scale * DOWN_W) * read(r, DOWN_K + 1)

        def get_up(r):
            return around(up, make_up, r)

        def get_down(r):
            return around(down, make_down, r)

        def get_up_c(r):
            if r not in up_c:
                up_c[r] = get_up(r) * up_rest
            return up_c[r]

        def get_down_c(r):
            if r not in down_c:
                down_c[r] = get_down(r) * down_rest
            return down_c[r]

        def make_quad(r, sign):
            here = read(r, 0)
            plus = get_up(r + sign * up_near) + get_up_c(r + sign * up_far)
            minus = get_down(r + sign * down_near) + get_down_c(r + sign * down_far)
            return (here * strength) * (here * (plus + minus) - plus * minus)

        def get_more(r):
            return around(more, lambda r: make_quad(r, 1), r)

        def get_less(r):
            return around(less, lambda r: make_quad(r, -1), r)

        for r in range(slabs):
            u_ref[r, pl.ds(base + PAD, ROWS), :] = (
                get_more(r - up_near) + get_less(r + up_near)
            ) + up_rest * (get_more(r - up_far) + get_less(r + up_far))
            d_ref[r, pl.ds(base + PAD, ROWS), :] = (
                get_more(r - down_near) + get_less(r + down_near)
            ) + down_rest * (get_more(r - down_far) + get_less(r + down_far))
            n_ref[r, pl.ds(base, ROWS), :] = own * (get_more(r) + get_less(r))

    def stage_b(kb):
        base = kb * ROWS
        decay = c_ref[pl.ds(base, ROWS), :]
        total = jnp.zeros((ROWS, LANES), jnp.float32)
        for r in range(slabs):
            here = e_ref[r, pl.ds(base + PAD, ROWS), :]
            rate = here * (w_ref[r, pl.ds(base, ROWS), :] - decay) + n_ref[r, pl.ds(base, ROWS), :]
            rate = rate + (
                u_ref[r, pl.ds(base + PAD - UP_K, ROWS), :]
                + up_tail * u_ref[r, pl.ds(base + PAD - UP_K - 1, ROWS), :]
            )
            rate = rate + (
                down_head * d_ref[r, pl.ds(base + PAD - DOWN_K, ROWS), :]
                + down_tail * d_ref[r, pl.ds(base + PAD - DOWN_K - 1, ROWS), :]
            )
            here = here + (LIMITER / SUB / GAIN) * jnp.tanh(rate)
            e_ref[r, pl.ds(base + PAD, ROWS), :] = here
            total = total + here
        acc_ref[pl.ds(base, ROWS), :] = total

    def sub_step(index, carry):
        steepness = jnp.sum(acc_ref[...] * table_ref[3], axis=0, keepdims=True)
        steepness = pack.over_blocks(jnp.broadcast_to(steepness, (ROWS, LANES)), lane)[0:1]
        c_ref[...] = steepness * table_ref[4]
        for kb in range(blocks):
            stage_a(kb)
        for kb in range(blocks):
            stage_b(kb)
        return carry

    lax.fori_loop(0, SUB, sub_step, 0)


def slab_at(r, kb, freq_count):
    return pl.ds(r * freq_count + kb * ROWS, ROWS)


SQUEEZE = (0, COAST, 4 * COAST, 5 * COAST)


def flow_mask(lane, width, wanted):
    block = lane // width
    forward = ((block == 0) | (block == 3)).astype(jnp.int32)
    return (forward == wanted) & (lane % width < COAST)


def squeeze(fetch, count, chosen):
    out = []
    for start in range(0, count, len(SQUEEZE)):
        total = None
        for i in range(start, min(count, start + len(SQUEEZE))):
            value = turn(jnp.where(chosen, fetch(i), 0.0), SQUEEZE[i - start])
            total = value if total is None else total + value
        out.append(total)
    return out


def loosen(ref, i):
    g, part = divmod(i, len(SQUEEZE))
    return turn(ref[pl.ds(g * ROWS, ROWS), :], -SQUEEZE[part])


def spread_kernel(
    one, two, freq_count, code_ref, spec_hbm, mask_hbm, wind_hbm, deal_hbm, table_ref,
    one_own, one_send, two_own, two_send, cross_ref, row_ref,
    spec_ref, mask_ref, wind_ref, deal_ref, moved_ref, sems,
):
    dir_count = one.dir_count
    blocks = freq_count // ROWS
    copies = [
        pltpu.make_async_copy(src, dst, sems.at[i])
        for i, (src, dst) in enumerate(
            [(mask_hbm, mask_ref), (wind_hbm, wind_ref), (deal_hbm, deal_ref), (spec_hbm, spec_ref)]
        )
    ]
    for copy in copies:
        copy.start()
    for copy in copies:
        copy.wait()
    lane = lanes()
    mask = mask_ref[...].astype(jnp.float32)
    half = mask * (1.0 / GAIN)
    parity = code_ref[0] % 2
    angles = 2.0 * math.pi * np.arange(dir_count) / dir_count

    aux = jnp.concatenate(
        [
            wind_ref[...] * mask,
            (deal_ref[...] + 1).astype(jnp.float32) * mask,
            mask,
            jnp.zeros((ROWS - 4, LANES), jnp.float32),
        ],
        axis=0,
    )
    row_ref[...] = jnp.concatenate(
        [mask, jnp.broadcast_to(mask[:, LANES - 1:LANES], (1, LANES)), jnp.zeros((ROWS - 2, LANES), jnp.float32)], axis=0
    )

    def pack_row(pack, values, first, slot, count):
        total = None
        for b, value in enumerate(values):
            at = b * pack.width + slot
            value = turn(value, at - first)
            keep = within(lane, at, count)
            total = jnp.where(keep, value, 0.0 if total is None else total)
        return total

    def put_aux(ref, pack, first, slot, count):
        ref[pl.ds(pack.slabs * freq_count, ROWS), :] = pack_row(pack, [aux] * pack.blocks, first, slot, count)

    put_aux(one_own, one, COAST + REST, 0, NEAR)
    put_aux(one_send, one, FAR, 0, NEAR)
    put_aux(two_own, two, 0, 0, COAST + REST)
    put_aux(two_send, two, FAR + NEAR, COAST, REST)

    def field(j, kb):
        return spec_ref[pl.ds(kb * ROWS * dir_count + j, ROWS, stride=dir_count), :] * mask

    for kb in range(blocks):
        speed = table_ref[0, pl.ds(kb * ROWS, ROWS), :]

        def move(j):
            here = field(j, kb)
            if sine_up(j, dir_count):
                along = jnp.where(lane == 0, 0.0, turn(here, 1))
            else:
                along = jnp.where(lane == LANES - 1, 0.0, turn(here, -1))
            moved = (
                here
                - speed * float(abs(math.cos(angles[j]))) * here
                - speed * float(abs(math.sin(angles[j]))) * (here - along)
            ) * half
            moved_ref[j, pl.ds(kb * ROWS, ROWS), :] = moved
            return moved

        for r in range(one.slabs):
            moved = [move(one.direction(b, r)) for b in range(one.blocks)]
            at = slab_at(r, kb, freq_count)
            one_own[at, :] = pack_row(one, moved, COAST + REST, 0, NEAR)
            one_send[at, :] = pack_row(one, moved, FAR, 0, NEAR)
        for r in range(two.slabs):
            at = slab_at(r, kb, freq_count)
            chosen = [two.direction(b, r) for b in range(two.blocks)]
            raw = pack_row(two, [field(j, kb) for j in chosen], 0, 0, two.width)
            two_own[at, :] = raw
            moved = [moved_ref[j, pl.ds(kb * ROWS, ROWS), :] for j in chosen]
            sent = pack_row(two, moved, FAR + NEAR, COAST, REST)
            two_send[at, :] = jnp.where(lane % two.width < COAST, raw, sent)

    def fetch(i):
        return two_own[pl.ds(i * ROWS, ROWS), :]

    chosen = flow_mask(lane, two.width, parity)
    for g, value in enumerate(squeeze(fetch, two.slabs * blocks, chosen)):
        cross_ref[pl.ds(g * ROWS, ROWS), :] = value


def take_column(pack, fetch, slot_up, slot_down, kb, lane):
    total = jnp.zeros((ROWS, LANES), jnp.float32)
    for r in range(pack.slabs):
        value = fetch(r, kb)
        for b in range(pack.blocks):
            j = pack.direction(b, r)
            at = b * pack.width + (slot_up if sine_up(j, pack.dir_count) else slot_down)
            total = jnp.where(lane == j, turn(value, j - at), total)
    return total


def store_state(pack, freq_count, e_ref, scale, out_ref):
    for r in range(pack.slabs):
        for kb in range(freq_count // ROWS):
            out_ref[slab_at(r, kb, freq_count), :] = e_ref[r, pl.ds(PAD + kb * ROWS, ROWS), :] * scale


def one_kernel(one, freq_count, last, table_ref, angle_ref, *refs):
    if last:
        row_ref, in_ref, local_ref, column_ref, out_ref, energy_ref = refs[:6]
        scratch = refs[6:]
    else:
        own_ref, got_ref, out_ref, column_ref = refs[:4]
        scratch = refs[4:]
    e_ref, u_ref, d_ref, n_ref, w_ref, acc_ref, c_ref = scratch
    blocks = freq_count // ROWS
    lane = lanes()
    for ref in (e_ref, u_ref, d_ref):
        clear(ref, one.slabs, freq_count)
    aux_at = pl.ds(one.slabs * freq_count, ROWS)
    if last:
        aux = in_ref[aux_at, :]
        owner = jnp.broadcast_to(row_ref[1:2, :], (ROWS, LANES)) > 0.5
        up = (lane >= 1) & (lane < one.dir_count // 2 + 1)
    else:
        aux = own_ref[aux_at, :] + got_ref[aux_at, :]
        out_ref[aux_at, :] = aux
    mask = aux[3:4]
    set_wind(one, freq_count, table_ref, angle_ref, aux, w_ref)
    for kb in range(blocks):
        at = pl.ds(kb * ROWS, ROWS)
        total = jnp.zeros((ROWS, LANES), jnp.float32)
        if last:
            speed = table_ref[0, at, :]
            beyond = jnp.where(up == owner, local_ref[at, :], column_ref[at, :])
        for r in range(one.slabs):
            if last:
                here = in_ref[slab_at(r, kb, freq_count), :]
                along = jnp.where(angle_ref[1, r:r + 1, :] > 0, turn(here, 1), turn(here, -1))
                for b in range(one.blocks):
                    j = one.direction(b, r)
                    to = b * one.width + (0 if sine_up(j, one.dir_count) else NEAR - 1)
                    along = jnp.where(lane == to, turn(beyond, to - j), along)
                start = (
                    here
                    - speed * angle_ref[2, r:r + 1, :] * here
                    - speed * angle_ref[3, r:r + 1, :] * (here - along)
                ) * (mask * (1.0 / GAIN))
            else:
                start = own_ref[slab_at(r, kb, freq_count), :] + got_ref[slab_at(r, kb, freq_count), :]
            e_ref[r, pl.ds(PAD + kb * ROWS, ROWS), :] = start
            total = total + start
        acc_ref[at, :] = total
    sub_steps(one, freq_count, table_ref, e_ref, u_ref, d_ref, n_ref, w_ref, acc_ref, c_ref)
    store_state(one, freq_count, e_ref, mask * GAIN, out_ref)
    if last:
        energy = jnp.sum(acc_ref[...], axis=0, keepdims=True) * (mask * GAIN / (freq_count * one.dir_count))
        energy_ref[...] = jnp.concatenate(
            [energy, aux[2:3] - 1.0, jnp.zeros((ROWS - 2, LANES), jnp.float32)], axis=0
        )
    else:
        for kb in range(blocks):
            column_ref[pl.ds(kb * ROWS, ROWS), :] = take_column(
                one, lambda r, kb: out_ref[slab_at(r, kb, freq_count), :], NEAR - 1, 0, kb, lane
            )


def two_kernel(two, freq_count, slot_count, last, code_ref, table_ref, angle_ref, row_ref, *refs):
    if last:
        in_ref, pair_ref, cross_ref, local_ref, other_ref, out_ref, energy_ref = refs[:7]
        scratch = refs[7:]
    else:
        own_ref, got_ref, cross_ref, out_ref, column_ref, pair_out, cross_out = refs[:7]
        scratch = refs[7:]
    e_ref, u_ref, d_ref, n_ref, w_ref, acc_ref, c_ref = scratch
    blocks = freq_count // ROWS
    lane = lanes()
    slot = lane % two.width
    for ref in (e_ref, u_ref, d_ref):
        clear(ref, two.slabs, freq_count)
    aux_at = pl.ds(two.slabs * freq_count, ROWS)
    parity = code_ref[0] % 2
    inner = (code_ref[0] < 2).astype(jnp.float32)
    owner = jnp.broadcast_to(row_ref[1:2, :], (ROWS, LANES)) > 0.5
    from_cross = flow_mask(lane, two.width, 1 - parity)
    from_pair = flow_mask(lane, two.width, parity)
    if last:
        aux = in_ref[aux_at, :]
        mask = aux[3:4]
    else:
        first = own_ref[aux_at, :]
        aux = first + got_ref[aux_at, :]
        out_ref[aux_at, :] = aux
        mask = first[3:4]
    set_wind(two, freq_count, table_ref, angle_ref, aux, w_ref)
    for kb in range(blocks):
        at = pl.ds(kb * ROWS, ROWS)
        speed = table_ref[0, at, :]
        total = jnp.zeros((ROWS, LANES), jnp.float32)
        for r in range(two.slabs):
            rows = slab_at(r, kb, freq_count)
            i = r * blocks + kb
            across = loosen(cross_ref, i) * inner
            if last:
                here = in_ref[rows, :]
                beside = loosen(pair_ref, i)
            else:
                here = own_ref[rows, :]
                beside = got_ref[rows, :]
            beside = jnp.where(from_cross, across, jnp.where(from_pair, beside, 0.0))
            along = jnp.where(angle_ref[1, r:r + 1, :] > 0, turn(here, 1), turn(here, -1))
            if last:
                beyond = local_ref[at, :]
                for b in range(two.blocks):
                    j = two.direction(b, r)
                    start = b * two.width
                    if sine_up(j, two.dir_count):
                        to = start + COAST
                        along = jnp.where((lane == to) & ~owner, turn(beyond, to - j), along)
                    else:
                        to = start + COAST + REST - 1
                        along = jnp.where((lane == to) & owner, turn(beyond, to - j), along)
                        along = jnp.where((lane == start + COAST - 1) & ~owner, 0.0, along)
            else:
                along = jnp.where((slot == 0) & (angle_ref[1, r:r + 1, :] > 0), 0.0, along)
            start = (
                here
                - speed * angle_ref[2, r:r + 1, :] * (here - beside)
                - speed * angle_ref[3, r:r + 1, :] * (here - along)
            ) * (mask * (1.0 / GAIN))
            if not last:
                start = start + jnp.where(slot >= COAST, got_ref[rows, :], 0.0)
            e_ref[r, pl.ds(PAD + kb * ROWS, ROWS), :] = start
            total = total + start
        acc_ref[at, :] = total
    sub_steps(two, freq_count, table_ref, e_ref, u_ref, d_ref, n_ref, w_ref, acc_ref, c_ref)
    scale = aux[3:4] * GAIN
    store_state(two, freq_count, e_ref, scale, out_ref)
    if last:
        energy = jnp.sum(acc_ref[...], axis=0, keepdims=True) * (scale / (freq_count * two.dir_count))
        total = None
        for energy, deal in ((energy, aux[2:3] - 1.0), (other_ref[0:1], other_ref[1:2])):
            deal = deal.astype(jnp.int32)
            cards = energy_ref.shape[0]
            card = lax.broadcasted_iota(jnp.int32, (cards, LANES), 0) * slot_count
            place = lax.broadcasted_iota(jnp.int32, (LANES, LANES), 0)
            to_card = jnp.where((deal >= card) & (deal < card + slot_count), energy, 0.0)
            to_slot = (lax.rem(jnp.maximum(deal, 0), slot_count) == place).astype(jnp.float32)
            part = lax.dot_general(
                to_card, to_slot, (((1,), (1,)), ((), ())),
                precision=lax.Precision.HIGHEST, preferred_element_type=jnp.float32,
            )
            total = part if total is None else total + part
        energy_ref[...] = total
    else:
        for kb in range(blocks):
            column_ref[pl.ds(kb * ROWS, ROWS), :] = take_column(
                two, lambda r, kb: out_ref[slab_at(r, kb, freq_count), :], COAST + REST - 1, COAST, kb, lane
            )
        for ref, wanted in ((pair_out, 1 - parity), (cross_out, parity)):
            chosen = flow_mask(lane, two.width, wanted)
            for g, value in enumerate(
                squeeze(lambda i: out_ref[pl.ds(i * ROWS, ROWS), :], two.slabs * blocks, chosen)
            ):
                ref[pl.ds(g * ROWS, ROWS), :] = value


def gather_kernel(one, two, freq_count, row_ref, one_ref, one_got, two_ref, two_got, out_ref):
    dir_count = one.dir_count
    lane = lanes()
    mask = row_ref[0:1, :]
    for kb in range(freq_count // ROWS):
        for j in range(dir_count):
            b, r = one.find(j)
            at = slab_at(r, kb, freq_count)
            shift = b * one.width
            value = turn(one_ref[at, :], COAST + REST - shift)
            value = jnp.where(lane < FAR, value, turn(one_got[at, :], FAR - shift))
            b, r = two.find(j)
            at = slab_at(r, kb, freq_count)
            shift = b * two.width
            value = jnp.where(lane < COAST + REST, turn(two_ref[at, :], -shift), value)
            value = jnp.where(lane >= FAR + NEAR, turn(two_got[at, :], FAR + NEAR - COAST - shift), value)
            out_ref[pl.ds(kb * ROWS * dir_count + j, ROWS, stride=dir_count), :] = value * mask


def coast_width(tile_count, cell_count):
    capacity = cell_count // tile_count
    spread = tile_count * (tile_count - 8) // 8
    return -(-spread // (tile_count - 1)) * capacity


def shards(spectrum, sea_mask, card_deal, wind):
    freq_count, dir_count, row_count, row_width = spectrum.shape
    cell_count = row_count * row_width
    tile_count = lax.axis_size("tile")
    slot_count = cell_count // 8
    assert row_count == 1 and cell_count == LANES and coast_width(tile_count, cell_count) <= COAST
    here = lax.axis_index("tile")
    at_end = (here == 0) | (here == tile_count - 1)
    code = (here % 2 + 2 * at_end.astype(jnp.int32)).astype(jnp.int32).reshape(1)
    one, two = Pack(3, NEAR, dir_count, 0), Pack(4, 32, dir_count, 1)
    table = jnp.asarray(tables(freq_count, dir_count))
    one_rows, two_rows = one.slabs * freq_count, two.slabs * freq_count
    squeezed = -(-two_rows // ROWS // len(SQUEEZE)) * ROWS

    def array(*shape):
        return jax.ShapeDtypeStruct(shape, jnp.float32)

    smem = pl.BlockSpec(memory_space=pltpu.SMEM)
    vmem = pl.BlockSpec(memory_space=pltpu.VMEM)
    hbm = pl.BlockSpec(memory_space=pl.ANY)

    def params(elements, steps=SUB):
        work = elements * LANES * steps
        return dict(
            compiler_params=pltpu.CompilerParams(vmem_limit_bytes=48 * 1024 * 1024),
            cost_estimate=pl.CostEstimate(flops=50 * work, bytes_accessed=4 * work, transcendentals=work),
        )

    def scratch(pack):
        padded = pltpu.VMEM((pack.slabs, freq_count + 2 * PAD, LANES), jnp.float32)
        plain = pltpu.VMEM((pack.slabs, freq_count, LANES), jnp.float32)
        column = pltpu.VMEM((freq_count, LANES), jnp.float32)
        return [padded, padded, padded, plain, plain, column, column]

    group_count = lax.axis_size("groups")
    chip_swap = []
    for g in range(group_count):
        for i in range(tile_count):
            other, there = g, (i + 1 if i % 2 else i - 1)
            if not 0 <= there < tile_count:
                other, there = (g ^ 1 if g ^ 1 < group_count else g), i
            chip_swap.append((g * tile_count + i, other * tile_count + there))

    def to_pair(value):
        return lax.ppermute(value, "tile", [(i, i ^ 1) for i in range(tile_count)])

    def to_next(value):
        return lax.ppermute(value, ("groups", "tile"), chip_swap)

    one_angles, two_angles = jnp.asarray(one.rows()), jnp.asarray(two.rows())
    one_own, one_send, two_own, two_send, cross, row = pl.pallas_call(
        functools.partial(spread_kernel, one, two, freq_count),
        out_shape=(
            array(one_rows + ROWS, LANES), array(one_rows + ROWS, LANES),
            array(two_rows + ROWS, LANES), array(two_rows + ROWS, LANES),
            array(squeezed, LANES), array(ROWS, LANES),
        ),
        in_specs=[smem, hbm, hbm, hbm, hbm, vmem],
        out_specs=(vmem,) * 6,
        scratch_shapes=[
            pltpu.VMEM((freq_count * dir_count, LANES), jnp.float32),
            pltpu.VMEM((1, LANES), jnp.int32),
            pltpu.VMEM((2, LANES), jnp.float32),
            pltpu.VMEM((1, LANES), jnp.int32),
            pltpu.VMEM((dir_count, freq_count, LANES), jnp.float32),
            pltpu.SemaphoreType.DMA((4,)),
        ],
        name="spread",
        **params(1440, 1),
    )(
        code, spectrum.reshape(freq_count * dir_count, cell_count), sea_mask,
        wind.reshape(2, cell_count), card_deal, table,
    )
    one_got = to_pair(one_send)
    cross_got = to_next(cross)
    two_got = to_pair(two_send)
    one_state, one_column = pl.pallas_call(
        functools.partial(one_kernel, one, freq_count, False),
        out_shape=(array(one_rows + ROWS, LANES), array(freq_count, LANES)),
        in_specs=[vmem] * 4,
        out_specs=(vmem,) * 2,
        scratch_shapes=scratch(one),
        name="first_one",
        **params(one_rows),
    )(table, one_angles, one_own, one_got)
    column_got = to_pair(one_column)
    two_state, two_column, pair, cross = pl.pallas_call(
        functools.partial(two_kernel, two, freq_count, slot_count, False),
        out_shape=(
            array(two_rows + ROWS, LANES), array(freq_count, LANES), array(squeezed, LANES), array(squeezed, LANES),
        ),
        in_specs=[smem] + [vmem] * 6,
        out_specs=(vmem,) * 4,
        scratch_shapes=scratch(two),
        name="first_two",
        **params(two_rows),
    )(code, table, two_angles, row, two_own, two_got, cross_got)
    cross_got = to_next(cross)
    pair_got = to_pair(pair)
    one_state, one_energy = pl.pallas_call(
        functools.partial(one_kernel, one, freq_count, True),
        out_shape=(array(one_rows, LANES), array(ROWS, LANES)),
        in_specs=[vmem] * 6,
        out_specs=(vmem,) * 2,
        scratch_shapes=scratch(one),
        name="second_one",
        **params(one_rows),
    )(table, one_angles, row, one_state, two_column, column_got)
    one_got = to_pair(one_state)
    two_state, energy = pl.pallas_call(
        functools.partial(two_kernel, two, freq_count, slot_count, True),
        out_shape=(array(two_rows, LANES), array(tile_count, LANES)),
        in_specs=[smem] + [vmem] * 8,
        out_specs=(vmem,) * 2,
        scratch_shapes=scratch(two),
        name="second_two",
        **params(two_rows),
    )(code, table, two_angles, row, two_state, pair_got, cross_got, one_column, one_energy)
    two_got = to_pair(two_state)
    out = pl.pallas_call(
        functools.partial(gather_kernel, one, two, freq_count),
        out_shape=array(freq_count * dir_count, LANES),
        in_specs=[vmem] * 5,
        out_specs=vmem,
        name="gather",
        **params(1440, 1),
    )(row, one_state, one_got, two_state, two_got)
    shared = lax.all_to_all(
        energy.reshape(tile_count, 1, LANES), "tile", split_axis=0, concat_axis=0, tiled=True
    )
    card_energy = jnp.sum(shared, axis=(0, 1))[:slot_count]
    return out.reshape(freq_count, dir_count, row_count, row_width), card_energy


def solution(mesh):
    placed = (
        P(None, None, ("groups", "tile"), None),
        P(("groups", "tile"), None),
        P(("groups", "tile"), None),
        P(None, ("groups", "tile"), None),
    )
    return jax.shard_map(
        shards,
        mesh=mesh,
        in_specs=placed,
        out_specs=(P(None, None, ("groups", "tile"), None), P(("groups", "tile"))),
        check_vma=False,
    )
```

time: 50.1 us -> 53.6 us (1.070)
  Pallas kernels: 24.8 us -> 29.3 us
  waiting for transfers between devices: 4.14 us -> 2.61 us
  blocking collectives: 12.5 us -> 11.5 us
  local copies, waits for them, and re-layouts: 1.78 us -> 2.7 us
  starting transfers between devices: 5.29 us -> 5.89 us
    pallas_call x3 -> x6, Pallas kernels: 24.8 us -> 29.3 us  [the longest x1 7.84 us: shards(): pl.pallas_call(functools.partial(one_kernel, one, freq_count, True), out_...]
    ppermute x4 -> x8, waiting for transfers between devices: 4.14 us -> 2.61 us  [the longest x2 2.6 us: to_next(): return lax.ppermute(value, ('groups', 'tile'), chip_swap)]
    all_to_all x1, blocking collectives: 12.5 us -> 11.5 us  [shards(): lax.all_to_all(energy.reshape(tile_count, 1, LANES), 'tile', split_axis=0...]
    unnamed x10 -> x16, local copies, waits for them, and re-layouts: 1.78 us -> 2.7 us
    ppermute x4 -> x8, starting transfers between devices: 5.29 us -> 5.89 us  [the longest x2 4.41 us: to_next(): return lax.ppermute(value, ('groups', 'tile'), chip_swap)]
  transfers between devices with their start and end apart: 4 -> 8, of which waited for: 2 -> 1; matrix products, arithmetic and copies ran while one was open for 0% -> 1% of each run, Pallas kernels for 0% -> 28%
where the time goes in v2:
time: 53.6 us; the launch traced here: 53.3 us
  Pallas kernels  29.3 us (55%)
  blocking collectives  11.5 us (21%)
  starting transfers between devices  5.89 us (11%)
  local copies, waits for them, and re-layouts  2.7 us (5%)
  waiting for transfers between devices  2.61 us (5%)
  between operations  0.73 us (1%)
  other arithmetic  0.54 us (1%)
    all_to_all x1, blocking collectives, shards(): lax.all_to_all(energy.reshape(tile_count, 1, LANES), 'tile', split_axis=0...  11.5 us
    pallas_call x1, Pallas kernels, shards(): pl.pallas_call(functools.partial(one_kernel, one, freq_count, True), out_...  7.84 us
    pallas_call x1, Pallas kernels, shards(): pl.pallas_call(functools.partial(one_kernel, one, freq_count, False), out...  7.73 us
    pallas_call x2, Pallas kernels, shards(): pl.pallas_call(functools.partial(two_kernel, two, freq_count, slot_count,...  6.99 us
    pallas_call x1, Pallas kernels, shards(): pl.pallas_call(functools.partial(spread_kernel, one, two, freq_count), ou...  5.1 us
    ppermute x2, starting transfers between devices, to_next(): return lax.ppermute(value, ('groups', 'tile'), chip_swap)  4.41 us
    unnamed x16, local copies, waits for them, and re-layouts  2.7 us
    ppermute x2, waiting for transfers between devices, to_next(): return lax.ppermute(value, ('groups', 'tile'), chip_swap)  2.6 us
  transfers between devices with their start and end apart: 8, of which 1 were waited for; matrix products, arithmetic and copies ran while one was open for 1% of the time, Pallas kernels for 28%

profile of v2, /device:TPU:0, one launch (start us, length us, event | category | flops | bytes accessed | tf_op | source)
XLA Modules:
  0.0 53.3 jit_solution(8711773148548866477)
XLA Ops:
  0.6 0.0 copy-start.5
  0.7 0.0 copy-start.3
  0.7 0.0 copy-start.4
  0.7 0.6 %copy-done.5 = s32[1,128]{1,0:T(1,128)S(1)} copy-done((s32[1,128]{1,0:T(1,128)S(1)}, s32[1,128]{1,0:T(1,128)}, u32[]{:S(2)}) %copy-start.5) | copy-done | bytes 536
  1.3 0.0 copy-done.3
  1.3 0.0 copy-done.4
  1.3 0.0 copy-start
  1.3 1.1 %copy-done = f32[40,36,1,128]{3,2,1,0:T(1,128)S(1)} copy-done((f32[40,36,1,128]{3,2,1,0:T(1,128)S(1)}, f32[40,36,1,128]{3,2,1,0:T(1,128)}, u32[]{:S(2)}) %copy-start) | copy-done | bytes 737304
  2.5 0.0 copy-start.1
  2.5 0.9 %copy-done.1 = f32[5,40,128]{2,1,0:T(8,128)S(1)} copy-done((f32[5,40,128]{2,1,0:T(8,128)S(1)}, f32[5,40,128]{2,1,0:T(8,128)}, u32[]{:S(2)}) %copy-start.1) | copy-done | bytes 102424
  3.4 0.0 copy-start.2
  3.4 0.0 copy-start.7
  3.4 5.1 %spread.1 = (f32[488,128]{1,0:T(8,128)S(1)}, f32[488,128]{1,0:T(8,128)S(1)}, f32[368,128]{1,0:T(8,128)S(1)}, f32[368,128]{1,0:T(8,128)S(1)}, f32[96,128]{1,0:T(8,128)S(1)}, /*index=5*/f32[8,128]{1,0:T(8,128)S(1)}) custom-call(s32[1]{0:T(128)} %bitcast.code_ref, f32[1440,128]{1,0:T(8,128)S(1)} %bitcast.8, s32[1,128]{1,0:T(1,128)S(1)} %copy-done.4, ...), custom_call_target="tpu_custom_call" | custom-call | flops 9216000 | bytes 737280 | tf_op jit(solution)/shard_map/spread/pallas_call | solution.py:634
  8.5 0.5 collective-permute-start
  9.0 0.1 collective-permute-start.1
  9.1 2.9 %collective-permute-start.2 = (f32[96,128]{1,0:T(8,128)S(1)}, f32[96,128]{1,0:T(8,128)S(1)}, u32[]{:S(2)}, u32[]{:S(2)}) collective-permute-start(f32[96,128]{1,0:T(8,128)S(1)} %get-tuple-element.24), channel_id=1, source_target_pairs={{0,16},{1,2},{2,1},{3,4},{4,3},{5,6},{6,5},{7,8},{8,7},{9,10},{10,... | collective-permute-start | bytes 147464 | tf_op jit(solution)/shard_map/ppermute | solution.py:631
  12.0 0.0 collective-permute-done.refs_1_
  12.0 0.0 copy-done.2
  12.0 0.0 copy-done.7
  12.0 0.0 copy-start.6
  12.0 7.7 %first_one.1 = (f32[488,128]{1,0:T(8,128)S(1)}, f32[40,128]{1,0:T(8,128)S(1)}) custom-call(f32[5,40,128]{2,1,0:T(8,128)S(1)} %copy-done.2, f32[4,16,128]{2,1,0:T(8,128)S(1)} %copy-done.7, f32[488,128]{1,0:T(8,128)S(1)} %get-tuple-element.19.refs_0_, f32[488,128]{1,0:T(8,128)S(1)} %collective-permute-done.refs_1_), custom_call_target="tpu_custom_call" | custom-call | flops 24576000 | bytes 1966080 | tf_op jit(solution)/shard_map/first_one/pallas_call | solution.py:660
  19.7 0.2 collective-permute-start.3
  19.9 0.0 collective-permute-done.2.refs_2_
  19.9 0.0 collective-permute-done.1.refs_1_
  20.0 0.0 copy-done.6
  20.0 3.4 %first_two.1 = (f32[368,128]{1,0:T(8,128)S(1)}, f32[40,128]{1,0:T(8,128)S(1)}, f32[96,128]{1,0:T(8,128)S(1)}, f32[96,128]{1,0:T(8,128)S(1)}) custom-call(s32[1]{0:T(128)} %bitcast.code_ref, f32[5,40,128]{2,1,0:T(8,128)S(1)} %copy-done.2, f32[4,16,128]{2,1,0:T(8,128)S(1)} %copy-done.6, f32[8,128]{1,0:T(8,128)S(1)} %get-tuple-element.18.row_ref.refs_0_, ...), custom_call_target="tpu_custom_call" | custom-call | flops 18432000 | bytes 1474560 | tf_op jit(solution)/shard_map/first_two/pallas_call | solution.py:670
  23.4 0.0 collective-permute-done.3.refs_3_
  23.4 7.8 %second_one.1 = (f32[480,128]{1,0:T(8,128)S(1)}, f32[8,128]{1,0:T(8,128)S(1)}) custom-call(f32[5,40,128]{2,1,0:T(8,128)S(1)} %copy-done.2, f32[4,16,128]{2,1,0:T(8,128)S(1)} %copy-done.7, f32[8,128]{1,0:T(8,128)S(1)} %get-tuple-element.18.row_ref.refs_0_, f32[488,128]{1,0:T(8,128)S(1)} %get-tuple-element.21.refs_1_, ...), custom_call_target="tpu_custom_call" | custom-call | flops 24576000 | bytes 1966080 | tf_op jit(solution)/shard_map/second_one/pallas_call | solution.py:683
  31.2 0.4 collective-permute-start.4
  31.7 0.1 collective-permute-start.5
  31.8 1.5 %collective-permute-start.6 = (f32[96,128]{1,0:T(8,128)S(1)}, f32[96,128]{1,0:T(8,128)S(1)}, u32[]{:S(2)}, u32[]{:S(2)}) collective-permute-start(f32[96,128]{1,0:T(8,128)S(1)} %get-tuple-element.30), channel_id=1, source_target_pairs={{0,16},{1,2},{2,1},{3,4},{4,3},{5,6},{6,5},{7,8},{8,7},{9,10},{10,... | collective-permute-start | bytes 147464 | tf_op jit(solution)/shard_map/ppermute | solution.py:631
  33.3 0.0 collective-permute-done.5.refs_1_
  33.3 2.6 %collective-permute-done.6.refs_2_ = f32[96,128]{1,0:T(8,128)S(1)} collective-permute-done((f32[96,128]{1,0:T(8,128)S(1)}, f32[96,128]{1,0:T(8,128)S(1)}, u32[]{:S(2)}, u32[]{:S(2)}) %collective-permute-start.6) | collective-permute-done | bytes 49184 | tf_op jit(solution)/shard_map/ppermute | solution.py:631
  35.9 3.6 %second_two.1 = (f32[360,128]{1,0:T(8,128)S(1)}, f32[16,128]{1,0:T(8,128)S(1)}) custom-call(s32[1]{0:T(128)} %bitcast.code_ref, f32[5,40,128]{2,1,0:T(8,128)S(1)} %copy-done.2, f32[4,16,128]{2,1,0:T(8,128)S(1)} %copy-done.6, f32[8,128]{1,0:T(8,128)S(1)} %get-tuple-element.18.row_ref.refs_0_, f32[368,128]{1,0:T(8,128)S(1)} %get-tuple-element.28.refs_0_, ...), custom_call_target="tpu_custom_call" | custom-call | flops 18432000 | bytes 1474560 | tf_op jit(solution)/shard_map/second_two/pallas_call | solution.py:693
  39.5 0.1 collective-permute-start.7
  39.6 11.5 %all_to_all.5 = f32[16,1,128]{2,1,0:T(1,128)S(1)} all-to-all(f32[16,1,128]{2,1,0:T(1,128)S(1)} %bitcast.9), channel_id=1, replica_groups=mesh['groups'=2,'tile'=16] {'tile'}, dimensions={0} | all-to-all | bytes 16384 | tf_op jit(solution)/shard_map/all_to_all | solution.py:711
  51.1 0.5 %reduce_sum.9 = f32[128]{0:T(128)} reduce(f32[16,1,128]{2,1,0:T(1,128)S(1)} %all_to_all.5, f32[]{:T(128)} %constant.28.clone.1), dimensions={0,1}, to_apply=%region_0.1 | reduce | flops 1920 | bytes 8708 | tf_op jit(solution)/shard_map/reduce_sum | solution.py:714
  51.7 0.0 collective-permute-done.7.two_got
  51.7 0.0 collective-permute-done.4.one_got
  51.7 1.6 %gather.1 = f32[1440,128]{1,0:T(8,128)} custom-call(f32[8,128]{1,0:T(8,128)S(1)} %get-tuple-element.18.row_ref.refs_0_, f32[480,128]{1,0:T(8,128)S(1)} %get-tuple-element.27.one_ref, f32[480,128]{1,0:T(8,128)S(1)} %collective-permute-done.4.one_got, f32[360,128]{1,0:T(8,128)S(1)} %get-tuple-element.32.two_ref, f32[360,128]{1,0:T(8,128)S(1)} %collective-permute-done.7.two_got), custom_call_target="tpu_custom_call" | custom-call | flops 9216000 | bytes 737280 | tf_op jit(solution)/shard_map/gather/pallas_call | solution.py:703
Async XLA Ops:
  0.6 0.7 %copy-start.5 = (s32[1,128]{1,0:T(1,128)S(1)}, s32[1,128]{1,0:T(1,128)}, u32[]{:S(2)}) copy-start(s32[1,128]{1,0:T(1,128)} %deal_hbm.1) | copy-start | bytes 1540
  0.7 0.7 %copy-start.3 = (f32[2,1,128]{2,1,0:T(1,128)S(1)}, f32[2,1,128]{2,1,0:T(1,128)}, u32[]{:S(2)}) copy-start(f32[2,1,128]{2,1,0:T(1,128)} %param.10) | copy-start | bytes 3076
  0.7 0.7 %copy-start.4 = (s32[1,128]{1,0:T(1,128)S(1)}, s32[1,128]{1,0:T(1,128)}, u32[]{:S(2)}) copy-start(s32[1,128]{1,0:T(1,128)} %mask_hbm.1) | copy-start | bytes 1540
  1.3 1.1 %copy-start = (f32[40,36,1,128]{3,2,1,0:T(1,128)S(1)}, f32[40,36,1,128]{3,2,1,0:T(1,128)}, u32[]{:S(2)}) copy-start(f32[40,36,1,128]{3,2,1,0:T(1,128)} %param.7) | copy-start | bytes 2211844
  2.5 0.9 %copy-start.1 = (f32[5,40,128]{2,1,0:T(8,128)S(1)}, f32[5,40,128]{2,1,0:T(8,128)}, u32[]{:S(2)}) copy-start(f32[5,40,128]{2,1,0:T(8,128)} %constant.29.clone.table_ref) | copy-start | bytes 307204
  3.4 8.6 %copy-start.2 = (f32[5,40,128]{2,1,0:T(8,128)S(1)}, f32[5,40,128]{2,1,0:T(8,128)}, u32[]{:S(2)}) copy-start(f32[5,40,128]{2,1,0:T(8,128)} %constant.29.clone.table_ref) | copy-start | bytes 307204
  3.4 8.6 %copy-start.7 = (f32[4,16,128]{2,1,0:T(8,128)S(1)}, f32[4,16,128]{2,1,0:T(8,128)}, u32[]{:S(2)}) copy-start(f32[4,16,128]{2,1,0:T(8,128)} %constant.30.clone.angle_ref) | copy-start | bytes 98308
  8.5 3.5 %collective-permute-start = (f32[488,128]{1,0:T(8,128)S(1)}, f32[488,128]{1,0:T(8,128)S(1)}, u32[]{:S(2)}, u32[]{:S(2)}) collective-permute-start(f32[488,128]{1,0:T(8,128)S(1)} %get-tuple-element.20), channel_id=1, source_target_pairs={{0,1},{1,0},{2,3},{3,2},{4,5},{5,4},{6,7},{7,6},{8,9},{9,8},{10,11... | collective-permute-start | bytes 749576 | tf_op jit(solution)/shard_map/ppermute | solution.py:628
  9.0 11.0 %collective-permute-start.1 = (f32[368,128]{1,0:T(8,128)S(1)}, f32[368,128]{1,0:T(8,128)S(1)}, u32[]{:S(2)}, u32[]{:S(2)}) collective-permute-start(f32[368,128]{1,0:T(8,128)S(1)} %get-tuple-element.23), channel_id=1, source_target_pairs={{0,1},{1,0},{2,3},{3,2},{4,5},{5,4},{6,7},{7,6},{8,9},{9,8},{10,11... | collective-permute-start | bytes 565256 | tf_op jit(solution)/shard_map/ppermute | solution.py:628
  9.1 10.9 %collective-permute-start.2 = (f32[96,128]{1,0:T(8,128)S(1)}, f32[96,128]{1,0:T(8,128)S(1)}, u32[]{:S(2)}, u32[]{:S(2)}) collective-permute-start(f32[96,128]{1,0:T(8,128)S(1)} %get-tuple-element.24), channel_id=1, source_target_pairs={{0,16},{1,2},{2,1},{3,4},{4,3},{5,6},{6,5},{7,8},{8,7},{9,10},{10,... | collective-permute-start | bytes 147464 | tf_op jit(solution)/shard_map/ppermute | solution.py:631
  12.0 8.0 %copy-start.6 = (f32[4,16,128]{2,1,0:T(8,128)S(1)}, f32[4,16,128]{2,1,0:T(8,128)}, u32[]{:S(2)}) copy-start(f32[4,16,128]{2,1,0:T(8,128)} %constant.31.clone.angle_ref) | copy-start | bytes 98308
  19.7 3.6 %collective-permute-start.3 = (f32[40,128]{1,0:T(8,128)S(1)}, f32[40,128]{1,0:T(8,128)S(1)}, u32[]{:S(2)}, u32[]{:S(2)}) collective-permute-start(f32[40,128]{1,0:T(8,128)S(1)} %get-tuple-element.26.refs_3_), channel_id=1, source_target_pairs={{0,1},{1,0},{2,3},{3,2},{4,5},{5,4},{6,7},{7,6},{8,9},{9,8},{10,11... | collective-permute-start | bytes 61448 | tf_op jit(solution)/shard_map/ppermute | solution.py:628
  31.2 20.4 %collective-permute-start.4 = (f32[480,128]{1,0:T(8,128)S(1)}, f32[480,128]{1,0:T(8,128)S(1)}, u32[]{:S(2)}, u32[]{:S(2)}) collective-permute-start(f32[480,128]{1,0:T(8,128)S(1)} %get-tuple-element.27.one_ref), channel_id=1, source_target_pairs={{0,1},{1,0},{2,3},{3,2},{4,5},{5,4},{6,7},{7,6},{8,9},{9,8},{10,11... | collective-permute-start | bytes 737288 | tf_op jit(solution)/shard_map/ppermute | solution.py:628
  31.7 1.6 %collective-permute-start.5 = (f32[96,128]{1,0:T(8,128)S(1)}, f32[96,128]{1,0:T(8,128)S(1)}, u32[]{:S(2)}, u32[]{:S(2)}) collective-permute-start(f32[96,128]{1,0:T(8,128)S(1)} %get-tuple-element.29), channel_id=1, source_target_pairs={{0,1},{1,0},{2,3},{3,2},{4,5},{5,4},{6,7},{7,6},{8,9},{9,8},{10,11... | collective-permute-start | bytes 147464 | tf_op jit(solution)/shard_map/ppermute | solution.py:628
  31.8 4.1 %collective-permute-start.6 = (f32[96,128]{1,0:T(8,128)S(1)}, f32[96,128]{1,0:T(8,128)S(1)}, u32[]{:S(2)}, u32[]{:S(2)}) collective-permute-start(f32[96,128]{1,0:T(8,128)S(1)} %get-tuple-element.30), channel_id=1, source_target_pairs={{0,16},{1,2},{2,1},{3,4},{4,3},{5,6},{6,5},{7,8},{8,7},{9,10},{10,... | collective-permute-start | bytes 147464 | tf_op jit(solution)/shard_map/ppermute | solution.py:631
  39.5 12.2 %collective-permute-start.7 = (f32[360,128]{1,0:T(8,128)S(1)}, f32[360,128]{1,0:T(8,128)S(1)}, u32[]{:S(2)}, u32[]{:S(2)}) collective-permute-start(f32[360,128]{1,0:T(8,128)S(1)} %get-tuple-element.32.two_ref), channel_id=1, source_target_pairs={{0,1},{1,0},{2,3},{3,2},{4,5},{5,4},{6,7},{7,6},{8,9},{9,8},{10,11... | collective-permute-start | bytes 552968 | tf_op jit(solution)/shard_map/ppermute | solution.py:628

commit v3 on v2

--- a/solution.py
+++ b/solution.py
@@ -57,18 +57,17 @@
         return divmod((j - self.offset) % self.dir_count, self.slabs)
 
     def next_block(self, value, lane):
+        if self.blocks * self.width == LANES:
+            return turn(value, -self.width)
         last = (self.blocks - 1) * self.width
-        ahead = turn(value, -self.width)
+        return jnp.take_along_axis(value, jnp.where(lane < last, lane + self.width, lane - last), axis=1)
+
+    def block_before(self, value, lane):
         if self.blocks * self.width == LANES:
-            return ahead
-        return jnp.where(lane < last, ahead, turn(value, last))
-
-    def block_before(self, value, lane):
+            return turn(value, self.width)
         last = (self.blocks - 1) * self.width
-        behind = turn(value, self.width)
-        if self.blocks * self.width == LANES:
-            return behind
-        return jnp.where(lane >= self.width, behind, turn(value, -last))
+        source = jnp.where(lane >= self.width, lane - self.width, lane + last)
+        return jnp.take_along_axis(value, jnp.minimum(source, LANES - 1), axis=1)
 
     def over_blocks(self, value, lane):
         if self.blocks == 4:
@@ -285,21 +284,22 @@
 
 
 def spread_kernel(
-    one, two, freq_count, code_ref, spec_hbm, mask_hbm, wind_hbm, deal_hbm, table_ref,
+    one, two, freq_count, code_ref, spec_hbm, mask_hbm, wind_hbm, deal_hbm, table_hbm,
     one_own, one_send, two_own, two_send, cross_ref, row_ref,
-    spec_ref, mask_ref, wind_ref, deal_ref, moved_ref, sems,
+    spec_ref, mask_ref, wind_ref, deal_ref, table_ref, raw_ref, moved_ref, sems,
 ):
     dir_count = one.dir_count
     blocks = freq_count // ROWS
-    copies = [
-        pltpu.make_async_copy(src, dst, sems.at[i])
-        for i, (src, dst) in enumerate(
-            [(mask_hbm, mask_ref), (wind_hbm, wind_ref), (deal_hbm, deal_ref), (spec_hbm, spec_ref)]
-        )
-    ]
+    chunk = ROWS * dir_count
+    pairs = [(mask_hbm, mask_ref), (wind_hbm, wind_ref), (deal_hbm, deal_ref), (table_hbm, table_ref)]
+    small = len(pairs)
+    for kb in range(blocks):
+        rows = pl.ds(kb * chunk, chunk)
+        pairs.append((spec_hbm.at[rows], spec_ref.at[rows]))
+    copies = [pltpu.make_async_copy(src, dst, sems.at[i]) for i, (src, dst) in enumerate(pairs)]
     for copy in copies:
         copy.start()
-    for copy in copies:
+    for copy in copies[:small]:
         copy.wait()
     lane = lanes()
     mask = mask_ref[...].astype(jnp.float32)
@@ -337,14 +337,13 @@
     put_aux(two_own, two, 0, 0, COAST + REST)
     put_aux(two_send, two, FAR + NEAR, COAST, REST)
 
-    def field(j, kb):
-        return spec_ref[pl.ds(kb * ROWS * dir_count + j, ROWS, stride=dir_count), :] * mask
-
     for kb in range(blocks):
+        copies[small + kb].wait()
         speed = table_ref[0, pl.ds(kb * ROWS, ROWS), :]
 
         def move(j):
-            here = field(j, kb)
+            here = spec_ref[pl.ds(kb * chunk + j, ROWS, stride=dir_count), :] * mask
+            raw_ref[j] = here
             if sine_up(j, dir_count):
                 along = jnp.where(lane == 0, 0.0, turn(here, 1))
             else:
@@ -354,7 +353,7 @@
                 - speed * float(abs(math.cos(angles[j]))) * here
                 - speed * float(abs(math.sin(angles[j]))) * (here - along)
             ) * half
-            moved_ref[j, pl.ds(kb * ROWS, ROWS), :] = moved
+            moved_ref[j] = moved
             return moved
 
         for r in range(one.slabs):
@@ -365,10 +364,9 @@
         for r in range(two.slabs):
             at = slab_at(r, kb, freq_count)
             chosen = [two.direction(b, r) for b in range(two.blocks)]
-            raw = pack_row(two, [field(j, kb) for j in chosen], 0, 0, two.width)
+            raw = pack_row(two, [raw_ref[j] for j in chosen], 0, 0, two.width)
             two_own[at, :] = raw
-            moved = [moved_ref[j, pl.ds(kb * ROWS, ROWS), :] for j in chosen]
-            sent = pack_row(two, moved, FAR + NEAR, COAST, REST)
+            sent = pack_row(two, [moved_ref[j] for j in chosen], FAR + NEAR, COAST, REST)
             two_send[at, :] = jnp.where(lane % two.width < COAST, raw, sent)
 
     def fetch(i):
@@ -600,13 +598,14 @@
 
     smem = pl.BlockSpec(memory_space=pltpu.SMEM)
     vmem = pl.BlockSpec(memory_space=pltpu.VMEM)
-    hbm = pl.BlockSpec(memory_space=pl.ANY)
-
-    def params(elements, steps=SUB):
-        work = elements * LANES * steps
+    hbm = pl.BlockSpec(memory_space=pltpu.HBM)
+
+    def params(rows, steps=SUB):
         return dict(
             compiler_params=pltpu.CompilerParams(vmem_limit_bytes=48 * 1024 * 1024),
-            cost_estimate=pl.CostEstimate(flops=50 * work, bytes_accessed=4 * work, transcendentals=work),
+            cost_estimate=pl.CostEstimate(
+                flops=rows // ROWS * steps * 8_000_000, bytes_accessed=8 * rows * LANES, transcendentals=0
+            ),
         )
 
     def scratch(pack):
@@ -638,15 +637,17 @@
             array(two_rows + ROWS, LANES), array(two_rows + ROWS, LANES),
             array(squeezed, LANES), array(ROWS, LANES),
         ),
-        in_specs=[smem, hbm, hbm, hbm, hbm, vmem],
+        in_specs=[smem] + [hbm] * 5,
         out_specs=(vmem,) * 6,
         scratch_shapes=[
             pltpu.VMEM((freq_count * dir_count, LANES), jnp.float32),
             pltpu.VMEM((1, LANES), jnp.int32),
             pltpu.VMEM((2, LANES), jnp.float32),
             pltpu.VMEM((1, LANES), jnp.int32),
-            pltpu.VMEM((dir_count, freq_count, LANES), jnp.float32),
-            pltpu.SemaphoreType.DMA((4,)),
+            pltpu.VMEM(table.shape, jnp.float32),
+            pltpu.VMEM((dir_count, ROWS, LANES), jnp.float32),
+            pltpu.VMEM((dir_count, ROWS, LANES), jnp.float32),
+            pltpu.SemaphoreType.DMA((4 + freq_count // ROWS,)),
         ],
         name="spread",
         **params(1440, 1),

time: 53.6 us -> 44 us (0.82)
  Pallas kernels: 29.3 us -> 22.4 us
  waiting for transfers between devices: 2.61 us -> 0.02 us
    pallas_call x1, Pallas kernels: 7.84 us -> 4.84 us  [shards(): pl.pallas_call(functools.partial(one_kernel, one, freq_count, True), out_...]
    pallas_call x1, Pallas kernels: 7.73 us -> 4.78 us  [shards(): pl.pallas_call(functools.partial(one_kernel, one, freq_count, False), out...]
    ppermute x2, waiting for transfers between devices: 2.6 us -> 0.01 us  [to_next(): return lax.ppermute(value, ('groups', 'tile'), chip_swap)]
    pallas_call x1, Pallas kernels: 5.1 us -> 4.18 us  [shards(): pl.pallas_call(functools.partial(spread_kernel, one, two, freq_count), ou...]
  transfers between devices with their start and end apart: 8 -> 8, of which waited for: 1 -> 0; matrix products, arithmetic and copies ran while one was open for 1% -> 1% of each run, Pallas kernels for 28% -> 38%
where the time goes in v3:
time: 44 us; the launch traced here: 43.8 us
  Pallas kernels  22.4 us (51%)
  blocking collectives  11.4 us (26%)
  starting transfers between devices  5.95 us (14%)
  local copies, waits for them, and re-layouts  2.7 us (6%)
  between operations  0.72 us (2%)
  other arithmetic  0.54 us (1%)
    all_to_all x1, blocking collectives, shards(): lax.all_to_all(energy.reshape(tile_count, 1, LANES), 'tile', split_axis=0...  11.4 us
    pallas_call x2, Pallas kernels, shards(): pl.pallas_call(functools.partial(two_kernel, two, freq_count, slot_count,...  6.99 us
    pallas_call x1, Pallas kernels, shards(): pl.pallas_call(functools.partial(one_kernel, one, freq_count, True), out_...  4.84 us
    pallas_call x1, Pallas kernels, shards(): pl.pallas_call(functools.partial(one_kernel, one, freq_count, False), out...  4.78 us
    pallas_call x1, Pallas kernels, shards(): pl.pallas_call(functools.partial(spread_kernel, one, two, freq_count), ou...  4.18 us
    ppermute x2, starting transfers between devices, to_next(): return lax.ppermute(value, ('groups', 'tile'), chip_swap)  4.05 us
    unnamed x16, local copies, waits for them, and re-layouts  2.7 us
    ppermute x6, starting transfers between devices, to_pair(): return lax.ppermute(value, 'tile', [(i, i ^ 1) for i in range(tile_count)])  1.9 us
  transfers between devices with their start and end apart: 8, of which 0 were waited for; matrix products, arithmetic and copies ran while one was open for 1% of the time, Pallas kernels for 38%

profile of v3, /device:TPU:0, one launch (start us, length us, event | category | flops | bytes accessed | tf_op | source)
XLA Modules:
  0.0 43.8 jit_solution(2805644481111935014)
XLA Ops:
  0.6 0.0 copy-start.3
  0.7 0.0 copy-start.1
  0.7 0.0 copy-start.2
  0.7 0.6 %copy-done.3 = s32[1,128]{1,0:T(1,128)S(1)} copy-done((s32[1,128]{1,0:T(1,128)S(1)}, s32[1,128]{1,0:T(1,128)}, u32[]{:S(2)}) %copy-start.3) | copy-done | bytes 536
  1.3 0.0 copy-done.1
  1.3 0.0 copy-done.2
  1.3 0.0 copy-start
  1.3 1.1 %copy-done = f32[40,36,1,128]{3,2,1,0:T(1,128)S(1)} copy-done((f32[40,36,1,128]{3,2,1,0:T(1,128)S(1)}, f32[40,36,1,128]{3,2,1,0:T(1,128)}, u32[]{:S(2)}) %copy-start) | copy-done | bytes 737304
  2.5 0.0 copy-start.4
  2.5 0.9 %copy-done.4 = f32[5,40,128]{2,1,0:T(8,128)S(1)} copy-done((f32[5,40,128]{2,1,0:T(8,128)S(1)}, f32[5,40,128]{2,1,0:T(8,128)}, u32[]{:S(2)}) %copy-start.4) | copy-done | bytes 102424
  3.4 0.0 copy-start.5
  3.4 0.0 copy-start.7
  3.4 4.2 %spread.1 = (f32[488,128]{1,0:T(8,128)S(1)}, f32[488,128]{1,0:T(8,128)S(1)}, f32[368,128]{1,0:T(8,128)S(1)}, f32[368,128]{1,0:T(8,128)S(1)}, f32[96,128]{1,0:T(8,128)S(1)}, /*index=5*/f32[8,128]{1,0:T(8,128)S(1)}) custom-call(s32[1]{0:T(128)} %bitcast.code_ref, f32[1440,128]{1,0:T(8,128)S(1)} %bitcast.9, s32[1,128]{1,0:T(1,128)S(1)} %copy-done.2, ...), custom_call_target="tpu_custom_call" | custom-call | flops 1440000000 | bytes 1474560 | tf_op jit(solution)/shard_map/spread/pallas_call | solution.py:633
  7.5 0.5 %collective-permute-start = (f32[488,128]{1,0:T(8,128)S(1)}, f32[488,128]{1,0:T(8,128)S(1)}, u32[]{:S(2)}, u32[]{:S(2)}) collective-permute-start(f32[488,128]{1,0:T(8,128)S(1)} %get-tuple-element.20), channel_id=1, source_target_pairs={{0,1},{1,0},{2,3},{3,2},{4,5},{5,4},{6,7},{7,6},{8,9},{9,8},{10,11... | collective-permute-start | bytes 749576 | tf_op jit(solution)/shard_map/ppermute | solution.py:627
  8.1 2.6 %collective-permute-start.2 = (f32[96,128]{1,0:T(8,128)S(1)}, f32[96,128]{1,0:T(8,128)S(1)}, u32[]{:S(2)}, u32[]{:S(2)}) collective-permute-start(f32[96,128]{1,0:T(8,128)S(1)} %get-tuple-element.24), channel_id=1, source_target_pairs={{0,16},{1,2},{2,1},{3,4},{4,3},{5,6},{6,5},{7,8},{8,7},{9,10},{10,... | collective-permute-start | bytes 147464 | tf_op jit(solution)/shard_map/ppermute | solution.py:630
  10.6 0.1 collective-permute-start.1
  10.8 0.0 collective-permute-done.refs_1_
  10.8 0.0 copy-done.5
  10.8 0.0 copy-done.7
  10.8 0.0 copy-start.6
  10.8 4.8 %first_one.1 = (f32[488,128]{1,0:T(8,128)S(1)}, f32[40,128]{1,0:T(8,128)S(1)}) custom-call(f32[5,40,128]{2,1,0:T(8,128)S(1)} %copy-done.5, f32[4,16,128]{2,1,0:T(8,128)S(1)} %copy-done.7, f32[488,128]{1,0:T(8,128)S(1)} %get-tuple-element.19.refs_0_, f32[488,128]{1,0:T(8,128)S(1)} %collective-permute-done.refs_1_), custom_call_target="tpu_custom_call" | custom-call | flops 3840000000 | bytes 491520 | tf_op jit(solution)/shard_map/first_one/pallas_call | solution.py:661
  15.6 0.4 collective-permute-start.3
  16.0 0.0 collective-permute-done.2.refs_2_
  16.0 0.0 collective-permute-done.1.refs_1_
  16.0 0.0 copy-done.6
  16.0 3.4 %first_two.1 = (f32[368,128]{1,0:T(8,128)S(1)}, f32[40,128]{1,0:T(8,128)S(1)}, f32[96,128]{1,0:T(8,128)S(1)}, f32[96,128]{1,0:T(8,128)S(1)}) custom-call(s32[1]{0:T(128)} %bitcast.code_ref, f32[5,40,128]{2,1,0:T(8,128)S(1)} %copy-done.5, f32[4,16,128]{2,1,0:T(8,128)S(1)} %copy-done.6, f32[8,128]{1,0:T(8,128)S(1)} %get-tuple-element.18.row_ref.refs_0_, ...), custom_call_target="tpu_custom_call" | custom-call | flops 2880000000 | bytes 368640 | tf_op jit(solution)/shard_map/first_two/pallas_call | solution.py:671
  19.4 0.2 collective-permute-start.5
  19.6 1.5 %collective-permute-start.6 = (f32[96,128]{1,0:T(8,128)S(1)}, f32[96,128]{1,0:T(8,128)S(1)}, u32[]{:S(2)}, u32[]{:S(2)}) collective-permute-start(f32[96,128]{1,0:T(8,128)S(1)} %get-tuple-element.30), channel_id=1, source_target_pairs={{0,16},{1,2},{2,1},{3,4},{4,3},{5,6},{6,5},{7,8},{8,7},{9,10},{10,... | collective-permute-start | bytes 147464 | tf_op jit(solution)/shard_map/ppermute | solution.py:630
  21.1 0.0 collective-permute-done.3.refs_3_
  21.1 4.8 %second_one.1 = (f32[480,128]{1,0:T(8,128)S(1)}, f32[8,128]{1,0:T(8,128)S(1)}) custom-call(f32[5,40,128]{2,1,0:T(8,128)S(1)} %copy-done.5, f32[4,16,128]{2,1,0:T(8,128)S(1)} %copy-done.7, f32[8,128]{1,0:T(8,128)S(1)} %get-tuple-element.18.row_ref.refs_0_, f32[488,128]{1,0:T(8,128)S(1)} %get-tuple-element.21.refs_1_, ...), custom_call_target="tpu_custom_call" | custom-call | flops 3840000000 | bytes 491520 | tf_op jit(solution)/shard_map/second_one/pallas_call | solution.py:684
  26.0 0.2 collective-permute-start.4
  26.2 0.0 collective-permute-done.5.refs_1_
  26.2 0.0 collective-permute-done.6.refs_2_
  26.2 3.6 %second_two.1 = (f32[360,128]{1,0:T(8,128)S(1)}, f32[16,128]{1,0:T(8,128)S(1)}) custom-call(s32[1]{0:T(128)} %bitcast.code_ref, f32[5,40,128]{2,1,0:T(8,128)S(1)} %copy-done.5, f32[4,16,128]{2,1,0:T(8,128)S(1)} %copy-done.6, f32[8,128]{1,0:T(8,128)S(1)} %get-tuple-element.18.row_ref.refs_0_, f32[368,128]{1,0:T(8,128)S(1)} %get-tuple-element.28.refs_0_, ...), custom_call_target="tpu_custom_call" | custom-call | flops 2880000000 | bytes 368640 | tf_op jit(solution)/shard_map/second_two/pallas_call | solution.py:694
  29.8 0.4 collective-permute-start.7
  30.2 11.4 %all_to_all.5 = f32[16,1,128]{2,1,0:T(1,128)S(1)} all-to-all(f32[16,1,128]{2,1,0:T(1,128)S(1)} %bitcast.8), channel_id=1, replica_groups=mesh['groups'=2,'tile'=16] {'tile'}, dimensions={0} | all-to-all | bytes 16384 | tf_op jit(solution)/shard_map/all_to_all | solution.py:712
  41.6 0.5 %reduce_sum.9 = f32[128]{0:T(128)} reduce(f32[16,1,128]{2,1,0:T(1,128)S(1)} %all_to_all.5, f32[]{:T(128)} %constant.28.clone.1), dimensions={0,1}, to_apply=%region_0.1 | reduce | flops 1920 | bytes 8708 | tf_op jit(solution)/shard_map/reduce_sum | solution.py:715
  42.1 0.0 collective-permute-done.7.two_got
  42.1 0.0 collective-permute-done.4.one_got
  42.1 1.6 %gather.1 = f32[1440,128]{1,0:T(8,128)} custom-call(f32[8,128]{1,0:T(8,128)S(1)} %get-tuple-element.18.row_ref.refs_0_, f32[480,128]{1,0:T(8,128)S(1)} %get-tuple-element.27.one_ref, f32[480,128]{1,0:T(8,128)S(1)} %collective-permute-done.4.one_got, f32[360,128]{1,0:T(8,128)S(1)} %get-tuple-element.32.two_ref, f32[360,128]{1,0:T(8,128)S(1)} %collective-permute-done.7.two_got), custom_call_target="tpu_custom_call" | custom-call | flops 1440000000 | bytes 1474560 | tf_op jit(solution)/shard_map/gather/pallas_call | solution.py:704
Async XLA Ops:
  0.6 0.7 %copy-start.3 = (s32[1,128]{1,0:T(1,128)S(1)}, s32[1,128]{1,0:T(1,128)}, u32[]{:S(2)}) copy-start(s32[1,128]{1,0:T(1,128)} %deal_hbm.1) | copy-start | bytes 1540
  0.7 0.7 %copy-start.1 = (f32[2,1,128]{2,1,0:T(1,128)S(1)}, f32[2,1,128]{2,1,0:T(1,128)}, u32[]{:S(2)}) copy-start(f32[2,1,128]{2,1,0:T(1,128)} %param.10) | copy-start | bytes 3076
  0.7 0.7 %copy-start.2 = (s32[1,128]{1,0:T(1,128)S(1)}, s32[1,128]{1,0:T(1,128)}, u32[]{:S(2)}) copy-start(s32[1,128]{1,0:T(1,128)} %mask_hbm.1) | copy-start | bytes 1540
  1.3 1.1 %copy-start = (f32[40,36,1,128]{3,2,1,0:T(1,128)S(1)}, f32[40,36,1,128]{3,2,1,0:T(1,128)}, u32[]{:S(2)}) copy-start(f32[40,36,1,128]{3,2,1,0:T(1,128)} %param.7) | copy-start | bytes 2211844
  2.5 0.9 %copy-start.4 = (f32[5,40,128]{2,1,0:T(8,128)S(1)}, f32[5,40,128]{2,1,0:T(8,128)}, u32[]{:S(2)}) copy-start(f32[5,40,128]{2,1,0:T(8,128)} %constant.29.clone.table_hbm.table_ref) | copy-start | bytes 307204
  3.4 7.4 %copy-start.5 = (f32[5,40,128]{2,1,0:T(8,128)S(1)}, f32[5,40,128]{2,1,0:T(8,128)}, u32[]{:S(2)}) copy-start(f32[5,40,128]{2,1,0:T(8,128)} %constant.29.clone.table_hbm.table_ref) | copy-start | bytes 307204
  3.4 7.4 %copy-start.7 = (f32[4,16,128]{2,1,0:T(8,128)S(1)}, f32[4,16,128]{2,1,0:T(8,128)}, u32[]{:S(2)}) copy-start(f32[4,16,128]{2,1,0:T(8,128)} %constant.30.clone.angle_ref) | copy-start | bytes 98308
  7.5 3.2 %collective-permute-start = (f32[488,128]{1,0:T(8,128)S(1)}, f32[488,128]{1,0:T(8,128)S(1)}, u32[]{:S(2)}, u32[]{:S(2)}) collective-permute-start(f32[488,128]{1,0:T(8,128)S(1)} %get-tuple-element.20), channel_id=1, source_target_pairs={{0,1},{1,0},{2,3},{3,2},{4,5},{5,4},{6,7},{7,6},{8,9},{9,8},{10,11... | collective-permute-start | bytes 749576 | tf_op jit(solution)/shard_map/ppermute | solution.py:627
  8.1 7.9 %collective-permute-start.2 = (f32[96,128]{1,0:T(8,128)S(1)}, f32[96,128]{1,0:T(8,128)S(1)}, u32[]{:S(2)}, u32[]{:S(2)}) collective-permute-start(f32[96,128]{1,0:T(8,128)S(1)} %get-tuple-element.24), channel_id=1, source_target_pairs={{0,16},{1,2},{2,1},{3,4},{4,3},{5,6},{6,5},{7,8},{8,7},{9,10},{10,... | collective-permute-start | bytes 147464 | tf_op jit(solution)/shard_map/ppermute | solution.py:630
  10.6 5.4 %collective-permute-start.1 = (f32[368,128]{1,0:T(8,128)S(1)}, f32[368,128]{1,0:T(8,128)S(1)}, u32[]{:S(2)}, u32[]{:S(2)}) collective-permute-start(f32[368,128]{1,0:T(8,128)S(1)} %get-tuple-element.23), channel_id=1, source_target_pairs={{0,1},{1,0},{2,3},{3,2},{4,5},{5,4},{6,7},{7,6},{8,9},{9,8},{10,11... | collective-permute-start | bytes 565256 | tf_op jit(solution)/shard_map/ppermute | solution.py:627
  10.8 5.2 %copy-start.6 = (f32[4,16,128]{2,1,0:T(8,128)S(1)}, f32[4,16,128]{2,1,0:T(8,128)}, u32[]{:S(2)}) copy-start(f32[4,16,128]{2,1,0:T(8,128)} %constant.31.clone.angle_ref) | copy-start | bytes 98308
  15.6 5.6 %collective-permute-start.3 = (f32[40,128]{1,0:T(8,128)S(1)}, f32[40,128]{1,0:T(8,128)S(1)}, u32[]{:S(2)}, u32[]{:S(2)}) collective-permute-start(f32[40,128]{1,0:T(8,128)S(1)} %get-tuple-element.26.refs_3_), channel_id=1, source_target_pairs={{0,1},{1,0},{2,3},{3,2},{4,5},{5,4},{6,7},{7,6},{8,9},{9,8},{10,11... | collective-permute-start | bytes 61448 | tf_op jit(solution)/shard_map/ppermute | solution.py:627
  19.4 6.8 %collective-permute-start.5 = (f32[96,128]{1,0:T(8,128)S(1)}, f32[96,128]{1,0:T(8,128)S(1)}, u32[]{:S(2)}, u32[]{:S(2)}) collective-permute-start(f32[96,128]{1,0:T(8,128)S(1)} %get-tuple-element.29), channel_id=1, source_target_pairs={{0,1},{1,0},{2,3},{3,2},{4,5},{5,4},{6,7},{7,6},{8,9},{9,8},{10,11... | collective-permute-start | bytes 147464 | tf_op jit(solution)/shard_map/ppermute | solution.py:627
  19.6 6.6 %collective-permute-start.6 = (f32[96,128]{1,0:T(8,128)S(1)}, f32[96,128]{1,0:T(8,128)S(1)}, u32[]{:S(2)}, u32[]{:S(2)}) collective-permute-start(f32[96,128]{1,0:T(8,128)S(1)} %get-tuple-element.30), channel_id=1, source_target_pairs={{0,16},{1,2},{2,1},{3,4},{4,3},{5,6},{6,5},{7,8},{8,7},{9,10},{10,... | collective-permute-start | bytes 147464 | tf_op jit(solution)/shard_map/ppermute | solution.py:630
  26.0 16.1 %collective-permute-start.4 = (f32[480,128]{1,0:T(8,128)S(1)}, f32[480,128]{1,0:T(8,128)S(1)}, u32[]{:S(2)}, u32[]{:S(2)}) collective-permute-start(f32[480,128]{1,0:T(8,128)S(1)} %get-tuple-element.27.one_ref), channel_id=1, source_target_pairs={{0,1},{1,0},{2,3},{3,2},{4,5},{5,4},{6,7},{7,6},{8,9},{9,8},{10,11... | collective-permute-start | bytes 737288 | tf_op jit(solution)/shard_map/ppermute | solution.py:627
  29.8 12.3 %collective-permute-start.7 = (f32[360,128]{1,0:T(8,128)S(1)}, f32[360,128]{1,0:T(8,128)S(1)}, u32[]{:S(2)}, u32[]{:S(2)}) collective-permute-start(f32[360,128]{1,0:T(8,128)S(1)} %get-tuple-element.32.two_ref), channel_id=1, source_target_pairs={{0,1},{1,0},{2,3},{3,2},{4,5},{5,4},{6,7},{7,6},{8,9},{9,8},{10,11... | collective-permute-start | bytes 552968 | tf_op jit(solution)/shard_map/ppermute | solution.py:627

commit v4 on v3

--- a/solution.py
+++ b/solution.py
@@ -35,6 +35,7 @@
 
 
 GAIN = 2.0 * GAIN_BOTH / (GAIN_UP * GAIN_DOWN)
+STATE = SUB / LIMITER
 UP_K, UP_W = split(SHIFT_UP)
 DOWN_K, DOWN_W = split(SHIFT_DOWN)
 
@@ -83,7 +84,7 @@
 
     def rows(self):
         angles = 2.0 * math.pi * np.arange(self.dir_count) / self.dir_count
-        out = np.zeros((4, 16, LANES))
+        out = np.zeros((4, self.slabs, LANES))
         for r in range(self.slabs):
             for b in range(self.blocks):
                 at = slice(b * self.width, (b + 1) * self.width)
@@ -91,7 +92,7 @@
                 out[:, r, at] = np.array(
                     [math.cos(angle), math.sin(angle), abs(math.cos(angle)), abs(math.sin(angle))]
                 )[:, None]
-        return out.astype(np.float32)
+        return np.broadcast_to(out[:, :, None, :], (4, self.slabs, ROWS, LANES)).astype(np.float32)
 
 
 def turn(value, by):
@@ -101,6 +102,10 @@
 
 def lanes():
     return lax.broadcasted_iota(jnp.int32, (ROWS, LANES), 1)
+
+
+def every_row(value, row):
+    return jnp.broadcast_to(value[row:row + 1, :], (ROWS, LANES))
 
 
 def within(lane, first, count):
@@ -118,10 +123,10 @@
     rate = (1.0 - UP_W) * up_z / LIMITER
     rows = [
         speeds,
-        rate * QUAD_RATE * GAIN * GAIN * levels,
-        GAIN / LIMITER * WIND_RATE * 0.5 * levels,
-        GAIN / (dir_count * np.sum(levels)) * levels,
-        GAIN / LIMITER * DECAY_RATE * levels,
+        rate * QUAD_RATE / (GAIN * STATE ** 3) * levels,
+        WIND_RATE * 0.5 / (LIMITER * STATE) * levels,
+        levels / (dir_count * np.sum(levels) * STATE),
+        DECAY_RATE / (LIMITER * STATE) * levels,
     ]
     return np.broadcast_to(
         np.stack(rows)[:, :, None], (len(rows), freq_count, LANES)
@@ -136,11 +141,12 @@
 
 
 def set_wind(pack, freq_count, table_ref, angle_ref, aux, w_ref):
+    east, north = every_row(aux, 0), every_row(aux, 1)
     for r in range(pack.slabs):
-        drive = aux[0:1] * angle_ref[0, r:r + 1, :] + aux[1:2] * angle_ref[1, r:r + 1, :]
+        drive = east * angle_ref[0, r] + north * angle_ref[1, r]
         for kb in range(freq_count // ROWS):
             at = pl.ds(kb * ROWS, ROWS)
-            w_ref[r, at, :] = jnp.maximum(table_ref[2, at, :] * drive - GAIN / LIMITER * WIND_RATE, 0.0)
+            w_ref[r, at, :] = jnp.maximum(table_ref[2, at, :] * drive - WIND_RATE / (LIMITER * STATE), 0.0)
 
 
 def sub_steps(pack, freq_count, table_ref, e_ref, u_ref, d_ref, n_ref, w_ref, acc_ref, c_ref):
@@ -212,7 +218,27 @@
         def get_less(r):
             return around(less, lambda r: make_quad(r, -1), r)
 
-        for r in range(slabs):
+        if slabs > 9:
+            for r in (slabs - 2, slabs - 1, 0, 1):
+                get_up(r)
+            for r in (*range(slabs - 4, slabs), *range(4)):
+                get_down(r)
+            for r in (-2, -1, slabs, slabs + 1):
+                get_up(r)
+            for r in (*range(-4, 0), *range(slabs, slabs + 4)):
+                get_down(r)
+            for r in (*range(slabs - 4, slabs), 0, 1):
+                get_more(r)
+            for r in (slabs - 2, slabs - 1, *range(4)):
+                get_less(r)
+            for r in (*range(-4, 0), slabs, slabs + 1):
+                get_more(r)
+            for r in (-2, -1, *range(slabs, slabs + 4)):
+                get_less(r)
+            order = (*range(4, slabs - 4), *range(4), *range(slabs - 4, slabs))
+        else:
+            order = range(slabs)
+        for r in order:
             u_ref[r, pl.ds(base + PAD, ROWS), :] = (
                 get_more(r - up_near) + get_less(r + up_near)
             ) + up_rest * (get_more(r - up_far) + get_less(r + up_far))
@@ -236,7 +262,7 @@
                 down_head * d_ref[r, pl.ds(base + PAD - DOWN_K, ROWS), :]
                 + down_tail * d_ref[r, pl.ds(base + PAD - DOWN_K - 1, ROWS), :]
             )
-            here = here + (LIMITER / SUB / GAIN) * jnp.tanh(rate)
+            here = here + jnp.tanh(rate)
             e_ref[r, pl.ds(base + PAD, ROWS), :] = here
             total = total + here
         acc_ref[pl.ds(base, ROWS), :] = total
@@ -283,30 +309,71 @@
     return turn(ref[pl.ds(g * ROWS, ROWS), :], -SQUEEZE[part])
 
 
-def spread_kernel(
-    one, two, freq_count, code_ref, spec_hbm, mask_hbm, wind_hbm, deal_hbm, table_hbm,
-    one_own, one_send, two_own, two_send, cross_ref, row_ref,
-    spec_ref, mask_ref, wind_ref, deal_ref, table_ref, raw_ref, moved_ref, sems,
-):
+def unpack_turn(value, pack):
+    return turn(value, -pack.width)
+
+
+def near_kernel(one, freq_count, spec_hbm, own_ref, send_ref, spec_ref, sems):
     dir_count = one.dir_count
     blocks = freq_count // ROWS
     chunk = ROWS * dir_count
-    pairs = [(mask_hbm, mask_ref), (wind_hbm, wind_ref), (deal_hbm, deal_ref), (table_hbm, table_ref)]
-    small = len(pairs)
+    copies = []
     for kb in range(blocks):
         rows = pl.ds(kb * chunk, chunk)
-        pairs.append((spec_hbm.at[rows], spec_ref.at[rows]))
-    copies = [pltpu.make_async_copy(src, dst, sems.at[i]) for i, (src, dst) in enumerate(pairs)]
-    for copy in copies:
-        copy.start()
-    for copy in copies[:small]:
-        copy.wait()
+        copies.append(pltpu.make_async_copy(spec_hbm.at[rows], spec_ref.at[rows], sems.at[kb]))
+        copies[kb].start()
     lane = lanes()
+    angles = 2.0 * math.pi * np.arange(dir_count) / dir_count
+    first = COAST + REST
+    row = lax.broadcasted_iota(jnp.int32, (ROWS, LANES), 0)
+    for kb in range(blocks):
+        copies[kb].wait()
+        speed = COURANT_TOP * STATE * jnp.exp((row + kb * ROWS).astype(jnp.float32) * (-math.log(1.1)))
+        for some in range(0, one.slabs, 4):
+            slabs = range(some, some + 4)
+            keys = [(r, b) for r in slabs for b in range(one.blocks)]
+            here = {
+                (r, b): spec_ref[pl.ds(kb * chunk + one.direction(b, r), ROWS, stride=dir_count), :] for r, b in keys
+            }
+            along, moved = {}, {}
+            for r, b in keys:
+                if sine_up(one.direction(b, r), dir_count):
+                    along[r, b] = turn(here[r, b], 1)
+                else:
+                    along[r, b] = jnp.where(lane == LANES - 1, 0.0, turn(here[r, b], -1))
+            for r, b in keys:
+                angle = angles[one.direction(b, r)]
+                cosine, sine = float(abs(math.cos(angle))), float(abs(math.sin(angle)))
+                value = here[r, b] * (STATE - speed * (cosine + sine)) + along[r, b] * (speed * sine)
+                moved[r, b] = turn(value, b * one.width - first)
+            own, sent = {}, {}
+            for r in slabs:
+                own[r] = sent[r] = moved[r, 0]
+                for b in range(1, one.blocks):
+                    at = b * one.width
+                    ahead = (at + one.width) % LANES
+                    own[r] = jnp.where(lane >= at, moved[r, b], own[r])
+                    reached = lane >= ahead
+                    if b == one.blocks - 1:
+                        reached = reached | (lane < one.width - (LANES - ahead))
+                    sent[r] = jnp.where(reached, moved[r, b], sent[r])
+            sent = {r: unpack_turn(sent[r], one) for r in slabs}
+            for r in slabs:
+                own_ref[slab_at(r, kb, freq_count), :] = own[r]
+                send_ref[slab_at(r, kb, freq_count), :] = sent[r]
+
+
+def pack_aux(pack, aux, first, slot, count):
+    lane = lanes()
+    total = jnp.zeros((ROWS, LANES), jnp.float32)
+    for b in range(pack.blocks):
+        at = b * pack.width + slot
+        total = jnp.where(within(lane, at, count), turn(aux, at - first), total)
+    return total
+
+
+def aux_kernel(one, two, mask_ref, wind_ref, deal_ref, row_ref, own_ref, send_ref):
     mask = mask_ref[...].astype(jnp.float32)
-    half = mask * (1.0 / GAIN)
-    parity = code_ref[0] % 2
-    angles = 2.0 * math.pi * np.arange(dir_count) / dir_count
-
     aux = jnp.concatenate(
         [
             wind_ref[...] * mask,
@@ -319,61 +386,44 @@
     row_ref[...] = jnp.concatenate(
         [mask, jnp.broadcast_to(mask[:, LANES - 1:LANES], (1, LANES)), jnp.zeros((ROWS - 2, LANES), jnp.float32)], axis=0
     )
-
-    def pack_row(pack, values, first, slot, count):
-        total = None
-        for b, value in enumerate(values):
-            at = b * pack.width + slot
-            value = turn(value, at - first)
-            keep = within(lane, at, count)
-            total = jnp.where(keep, value, 0.0 if total is None else total)
-        return total
-
-    def put_aux(ref, pack, first, slot, count):
-        ref[pl.ds(pack.slabs * freq_count, ROWS), :] = pack_row(pack, [aux] * pack.blocks, first, slot, count)
-
-    put_aux(one_own, one, COAST + REST, 0, NEAR)
-    put_aux(one_send, one, FAR, 0, NEAR)
-    put_aux(two_own, two, 0, 0, COAST + REST)
-    put_aux(two_send, two, FAR + NEAR, COAST, REST)
-
+    own_ref[pl.ds(0, ROWS), :] = pack_aux(one, aux, COAST + REST, 0, NEAR)
+    own_ref[pl.ds(ROWS, ROWS), :] = pack_aux(two, aux, 0, 0, COAST + REST)
+    send_ref[pl.ds(0, ROWS), :] = pack_aux(one, aux, FAR, 0, NEAR)
+    send_ref[pl.ds(ROWS, ROWS), :] = pack_aux(two, aux, FAR + NEAR, COAST, REST)
+
+
+def coast_kernel(two, freq_count, code_ref, spec_hbm, row_ref, own_ref, send_ref, cross_ref, spec_ref, sems):
+    dir_count = two.dir_count
+    blocks = freq_count // ROWS
+    chunk = ROWS * dir_count
+    copies = []
     for kb in range(blocks):
-        copies[small + kb].wait()
-        speed = table_ref[0, pl.ds(kb * ROWS, ROWS), :]
-
-        def move(j):
-            here = spec_ref[pl.ds(kb * chunk + j, ROWS, stride=dir_count), :] * mask
-            raw_ref[j] = here
-            if sine_up(j, dir_count):
-                along = jnp.where(lane == 0, 0.0, turn(here, 1))
-            else:
-                along = jnp.where(lane == LANES - 1, 0.0, turn(here, -1))
-            moved = (
-                here
-                - speed * float(abs(math.cos(angles[j]))) * here
-                - speed * float(abs(math.sin(angles[j]))) * (here - along)
-            ) * half
-            moved_ref[j] = moved
-            return moved
-
-        for r in range(one.slabs):
-            moved = [move(one.direction(b, r)) for b in range(one.blocks)]
-            at = slab_at(r, kb, freq_count)
-            one_own[at, :] = pack_row(one, moved, COAST + REST, 0, NEAR)
-            one_send[at, :] = pack_row(one, moved, FAR, 0, NEAR)
+        rows = pl.ds(kb * chunk, chunk)
+        copies.append(pltpu.make_async_copy(spec_hbm.at[rows], spec_ref.at[rows], sems.at[kb]))
+        copies[kb].start()
+    lane = lanes()
+    slot = lane % two.width
+    mask = every_row(row_ref[...], 0)
+    for kb in range(blocks):
+        copies[kb].wait()
+        done = []
         for r in range(two.slabs):
-            at = slab_at(r, kb, freq_count)
-            chosen = [two.direction(b, r) for b in range(two.blocks)]
-            raw = pack_row(two, [raw_ref[j] for j in chosen], 0, 0, two.width)
-            two_own[at, :] = raw
-            sent = pack_row(two, [moved_ref[j] for j in chosen], FAR + NEAR, COAST, REST)
-            two_send[at, :] = jnp.where(lane % two.width < COAST, raw, sent)
-
-    def fetch(i):
-        return two_own[pl.ds(i * ROWS, ROWS), :]
-
-    chosen = flow_mask(lane, two.width, parity)
-    for g, value in enumerate(squeeze(fetch, two.slabs * blocks, chosen)):
+            own, sent = None, None
+            for b in range(two.blocks):
+                j = two.direction(b, r)
+                here = spec_ref[pl.ds(kb * chunk + j, ROWS, stride=dir_count), :] * mask
+                here = turn(here, b * two.width)
+                block = within(lane, b * two.width, two.width)
+                behind = within(lane, (b - 1) % two.blocks * two.width, two.width)
+                own = here if b == 0 else jnp.where(block, here, own)
+                sent = here if b == 0 else jnp.where(behind, here, sent)
+            done.append((own, jnp.where(slot < COAST, own, sent)))
+        for r, (own, sent) in enumerate(done):
+            own_ref[slab_at(r, kb, freq_count), :] = own
+            send_ref[slab_at(r, kb, freq_count), :] = sent
+
+    chosen = flow_mask(lane, two.width, code_ref[0] % 2)
+    for g, value in enumerate(squeeze(lambda i: own_ref[pl.ds(i * ROWS, ROWS), :], two.slabs * blocks, chosen)):
         cross_ref[pl.ds(g * ROWS, ROWS), :] = value
 
 
@@ -390,8 +440,10 @@
 
 def store_state(pack, freq_count, e_ref, scale, out_ref):
     for r in range(pack.slabs):
-        for kb in range(freq_count // ROWS):
-            out_ref[slab_at(r, kb, freq_count), :] = e_ref[r, pl.ds(PAD + kb * ROWS, ROWS), :] * scale
+        blocks = range(freq_count // ROWS)
+        done = [e_ref[r, pl.ds(PAD + kb * ROWS, ROWS), :] * scale for kb in blocks]
+        for kb in blocks:
+            out_ref[slab_at(r, kb, freq_count), :] = done[kb]
 
 
 def one_kernel(one, freq_count, last, table_ref, angle_ref, *refs):
@@ -399,22 +451,23 @@
         row_ref, in_ref, local_ref, column_ref, out_ref, energy_ref = refs[:6]
         scratch = refs[6:]
     else:
-        own_ref, got_ref, out_ref, column_ref = refs[:4]
-        scratch = refs[4:]
-    e_ref, u_ref, d_ref, n_ref, w_ref, acc_ref, c_ref = scratch
+        row_ref, own_ref, got_ref, own_aux, got_aux, out_ref, column_ref = refs[:7]
+        scratch = refs[7:]
+    e_ref, u_ref, d_ref, n_ref, w_ref, acc_ref, c_ref, known_ref = scratch
+    known_ref[...] = table_ref[...]
     blocks = freq_count // ROWS
     lane = lanes()
     for ref in (e_ref, u_ref, d_ref):
         clear(ref, one.slabs, freq_count)
     aux_at = pl.ds(one.slabs * freq_count, ROWS)
+    owner = jnp.broadcast_to(row_ref[1:2, :], (ROWS, LANES)) > 0.5
     if last:
         aux = in_ref[aux_at, :]
-        owner = jnp.broadcast_to(row_ref[1:2, :], (ROWS, LANES)) > 0.5
         up = (lane >= 1) & (lane < one.dir_count // 2 + 1)
     else:
-        aux = own_ref[aux_at, :] + got_ref[aux_at, :]
+        aux = jnp.where(owner, own_aux[pl.ds(0, ROWS), :], got_aux[pl.ds(0, ROWS), :])
         out_ref[aux_at, :] = aux
-    mask = aux[3:4]
+    mask = every_row(aux, 3)
     set_wind(one, freq_count, table_ref, angle_ref, aux, w_ref)
     for kb in range(blocks):
         at = pl.ds(kb * ROWS, ROWS)
@@ -422,28 +475,35 @@
         if last:
             speed = table_ref[0, at, :]
             beyond = jnp.where(up == owner, local_ref[at, :], column_ref[at, :])
+        done = []
+        if last:
+            state = [in_ref[slab_at(r, kb, freq_count), :] for r in range(one.slabs)]
+            below = [turn(value, 1) for value in state]
+            above = [turn(value, -1) for value in state]
         for r in range(one.slabs):
             if last:
-                here = in_ref[slab_at(r, kb, freq_count), :]
-                along = jnp.where(angle_ref[1, r:r + 1, :] > 0, turn(here, 1), turn(here, -1))
+                here = state[r]
+                along = jnp.where(angle_ref[1, r] > 0, below[r], above[r])
                 for b in range(one.blocks):
                     j = one.direction(b, r)
                     to = b * one.width + (0 if sine_up(j, one.dir_count) else NEAR - 1)
                     along = jnp.where(lane == to, turn(beyond, to - j), along)
                 start = (
                     here
-                    - speed * angle_ref[2, r:r + 1, :] * here
-                    - speed * angle_ref[3, r:r + 1, :] * (here - along)
-                ) * (mask * (1.0 / GAIN))
+                    - speed * angle_ref[2, r] * here
+                    - speed * angle_ref[3, r] * (here - along)
+                ) * (mask * STATE)
             else:
-                start = own_ref[slab_at(r, kb, freq_count), :] + got_ref[slab_at(r, kb, freq_count), :]
+                start = jnp.where(owner, own_ref[slab_at(r, kb, freq_count), :], got_ref[slab_at(r, kb, freq_count), :])
+            done.append(start)
+            total = total + start
+        for r, start in enumerate(done):
             e_ref[r, pl.ds(PAD + kb * ROWS, ROWS), :] = start
-            total = total + start
         acc_ref[at, :] = total
-    sub_steps(one, freq_count, table_ref, e_ref, u_ref, d_ref, n_ref, w_ref, acc_ref, c_ref)
-    store_state(one, freq_count, e_ref, mask * GAIN, out_ref)
+    sub_steps(one, freq_count, known_ref, e_ref, u_ref, d_ref, n_ref, w_ref, acc_ref, c_ref)
+    store_state(one, freq_count, e_ref, mask * (1.0 / STATE), out_ref)
     if last:
-        energy = jnp.sum(acc_ref[...], axis=0, keepdims=True) * (mask * GAIN / (freq_count * one.dir_count))
+        energy = jnp.sum(acc_ref[...], axis=0, keepdims=True) * (mask[0:1] * (1.0 / (STATE * freq_count * one.dir_count)))
         energy_ref[...] = jnp.concatenate(
             [energy, aux[2:3] - 1.0, jnp.zeros((ROWS - 2, LANES), jnp.float32)], axis=0
         )
@@ -459,9 +519,10 @@
         in_ref, pair_ref, cross_ref, local_ref, other_ref, out_ref, energy_ref = refs[:7]
         scratch = refs[7:]
     else:
-        own_ref, got_ref, cross_ref, out_ref, column_ref, pair_out, cross_out = refs[:7]
-        scratch = refs[7:]
-    e_ref, u_ref, d_ref, n_ref, w_ref, acc_ref, c_ref = scratch
+        own_ref, got_ref, own_aux, got_aux, cross_ref, out_ref, column_ref, pair_out, cross_out = refs[:9]
+        scratch = refs[9:]
+    e_ref, u_ref, d_ref, n_ref, w_ref, acc_ref, c_ref, known_ref = scratch
+    known_ref[...] = table_ref[...]
     blocks = freq_count // ROWS
     lane = lanes()
     slot = lane % two.width
@@ -475,29 +536,37 @@
     from_pair = flow_mask(lane, two.width, parity)
     if last:
         aux = in_ref[aux_at, :]
-        mask = aux[3:4]
+        mask = every_row(aux, 3)
     else:
-        first = own_ref[aux_at, :]
-        aux = first + got_ref[aux_at, :]
+        second = pl.ds(ROWS, ROWS)
+        aux = own_aux[second, :] + got_aux[second, :]
         out_ref[aux_at, :] = aux
-        mask = first[3:4]
+        mask, got_mask = every_row(own_aux[second, :], 3), every_row(got_aux[second, :], 3)
     set_wind(two, freq_count, table_ref, angle_ref, aux, w_ref)
     for kb in range(blocks):
         at = pl.ds(kb * ROWS, ROWS)
         speed = table_ref[0, at, :]
         total = jnp.zeros((ROWS, LANES), jnp.float32)
-        for r in range(two.slabs):
-            rows = slab_at(r, kb, freq_count)
-            i = r * blocks + kb
-            across = loosen(cross_ref, i) * inner
-            if last:
-                here = in_ref[rows, :]
-                beside = loosen(pair_ref, i)
-            else:
-                here = own_ref[rows, :]
-                beside = got_ref[rows, :]
-            beside = jnp.where(from_cross, across, jnp.where(from_pair, beside, 0.0))
-            along = jnp.where(angle_ref[1, r:r + 1, :] > 0, turn(here, 1), turn(here, -1))
+        done = []
+        slabs = range(two.slabs)
+        upward = [angle_ref[1, r] > 0 for r in slabs]
+        flow_x = [speed * angle_ref[2, r] for r in slabs]
+        flow_y = [speed * angle_ref[3, r] for r in slabs]
+
+        def neighbours(values):
+            below = [turn(value, 1) for value in values]
+            above = [turn(value, -1) for value in values]
+            return [jnp.where(upward[r], below[r], above[r]) for r in slabs]
+
+        here = [(in_ref if last else own_ref)[slab_at(r, kb, freq_count), :] for r in slabs]
+        along = neighbours(here)
+        across = [loosen(cross_ref, r * blocks + kb) * inner for r in slabs]
+        if last:
+            beside = [loosen(pair_ref, r * blocks + kb) for r in slabs]
+        else:
+            beside = [got_ref[slab_at(r, kb, freq_count), :] for r in slabs]
+        for r in slabs:
+            nearby = jnp.where(from_cross, across[r], jnp.where(from_pair, beside[r], 0.0))
             if last:
                 beyond = local_ref[at, :]
                 for b in range(two.blocks):
@@ -505,28 +574,34 @@
                     start = b * two.width
                     if sine_up(j, two.dir_count):
                         to = start + COAST
-                        along = jnp.where((lane == to) & ~owner, turn(beyond, to - j), along)
+                        along[r] = jnp.where((lane == to) & ~owner, turn(beyond, to - j), along[r])
                     else:
                         to = start + COAST + REST - 1
-                        along = jnp.where((lane == to) & owner, turn(beyond, to - j), along)
-                        along = jnp.where((lane == start + COAST - 1) & ~owner, 0.0, along)
+                        along[r] = jnp.where((lane == to) & owner, turn(beyond, to - j), along[r])
+                        along[r] = jnp.where((lane == start + COAST - 1) & ~owner, 0.0, along[r])
             else:
-                along = jnp.where((slot == 0) & (angle_ref[1, r:r + 1, :] > 0), 0.0, along)
-            start = (
-                here
-                - speed * angle_ref[2, r:r + 1, :] * (here - beside)
-                - speed * angle_ref[3, r:r + 1, :] * (here - along)
-            ) * (mask * (1.0 / GAIN))
-            if not last:
-                start = start + jnp.where(slot >= COAST, got_ref[rows, :], 0.0)
+                along[r] = jnp.where((slot == 0) & upward[r], 0.0, along[r])
+            done.append(
+                (here[r] - flow_x[r] * (here[r] - nearby) - flow_y[r] * (here[r] - along[r])) * (mask * STATE)
+            )
+        if not last:
+            here = [turn(beside[r], COAST + REST) for r in slabs]
+            along = neighbours(here)
+            for r in slabs:
+                nearby = jnp.where((slot == COAST + REST - 1) & ~upward[r], 0.0, along[r])
+                done[r] = done[r] + (
+                    here[r] - flow_x[r] * here[r] - flow_y[r] * (here[r] - nearby)
+                ) * (got_mask * STATE)
+        for r in slabs:
+            total = total + done[r]
+        for r, start in enumerate(done):
             e_ref[r, pl.ds(PAD + kb * ROWS, ROWS), :] = start
-            total = total + start
         acc_ref[at, :] = total
-    sub_steps(two, freq_count, table_ref, e_ref, u_ref, d_ref, n_ref, w_ref, acc_ref, c_ref)
-    scale = aux[3:4] * GAIN
+    sub_steps(two, freq_count, known_ref, e_ref, u_ref, d_ref, n_ref, w_ref, acc_ref, c_ref)
+    scale = every_row(aux, 3) * (1.0 / STATE)
     store_state(two, freq_count, e_ref, scale, out_ref)
     if last:
-        energy = jnp.sum(acc_ref[...], axis=0, keepdims=True) * (scale / (freq_count * two.dir_count))
+        energy = jnp.sum(acc_ref[...], axis=0, keepdims=True) * (scale[0:1] / (freq_count * two.dir_count))
         total = None
         for energy, deal in ((energy, aux[2:3] - 1.0), (other_ref[0:1], other_ref[1:2])):
             deal = deal.astype(jnp.int32)
@@ -554,23 +629,39 @@
                 ref[pl.ds(g * ROWS, ROWS), :] = value
 
 
-def gather_kernel(one, two, freq_count, row_ref, one_ref, one_got, two_ref, two_got, out_ref):
+def gather_kernel(
+    one, two, freq_count, row_ref, one_ref, one_got, two_ref, two_got, shared_ref, out_hbm, energy_ref, out_ref, sems
+):
     dir_count = one.dir_count
+    chunk = ROWS * dir_count
     lane = lanes()
-    mask = row_ref[0:1, :]
+    mask = every_row(row_ref[...], 0)
+    energy_ref[...] = jnp.sum(shared_ref[...], axis=0, keepdims=True)[:, :energy_ref.shape[1]]
+    copies = []
     for kb in range(freq_count // ROWS):
-        for j in range(dir_count):
-            b, r = one.find(j)
-            at = slab_at(r, kb, freq_count)
-            shift = b * one.width
-            value = turn(one_ref[at, :], COAST + REST - shift)
-            value = jnp.where(lane < FAR, value, turn(one_got[at, :], FAR - shift))
-            b, r = two.find(j)
-            at = slab_at(r, kb, freq_count)
-            shift = b * two.width
-            value = jnp.where(lane < COAST + REST, turn(two_ref[at, :], -shift), value)
-            value = jnp.where(lane >= FAR + NEAR, turn(two_got[at, :], FAR + NEAR - COAST - shift), value)
-            out_ref[pl.ds(kb * ROWS * dir_count + j, ROWS, stride=dir_count), :] = value * mask
+        near = [turn(one_got[slab_at(r, kb, freq_count), :], one.width) for r in range(one.slabs)]
+        coast = [turn(two_got[slab_at(r, kb, freq_count), :], -(COAST + REST)) for r in range(two.slabs)]
+        for some in range(0, dir_count, 12):
+            js = range(some, some + 12)
+            value, rest = {}, {}
+            for j in js:
+                b, r = one.find(j)
+                start = b * one.width
+                mixed = jnp.where(within(lane, start, one.width), one_ref[slab_at(r, kb, freq_count), :], near[r])
+                value[j] = turn(mixed, COAST + REST - start)
+            for j in js:
+                b, r = two.find(j)
+                start = b * two.width
+                mixed = jnp.where(within(lane, start, COAST + REST), two_ref[slab_at(r, kb, freq_count), :], coast[r])
+                rest[j] = turn(mixed, -start)
+            for j in js:
+                whole = jnp.where(within(lane, COAST + REST, 2 * NEAR), value[j], rest[j]) * mask
+                out_ref[pl.ds(kb * chunk + j, ROWS, stride=dir_count), :] = whole
+        rows = pl.ds(kb * chunk, chunk)
+        copies.append(pltpu.make_async_copy(out_ref.at[rows], out_hbm.at[rows], sems.at[kb]))
+        copies[kb].start()
+    for copy in copies:
+        copy.wait()
 
 
 def coast_width(tile_count, cell_count):
@@ -600,9 +691,9 @@
     vmem = pl.BlockSpec(memory_space=pltpu.VMEM)
     hbm = pl.BlockSpec(memory_space=pltpu.HBM)
 
-    def params(rows, steps=SUB):
+    def params(rows, steps=SUB, vmem=48):
         return dict(
-            compiler_params=pltpu.CompilerParams(vmem_limit_bytes=48 * 1024 * 1024),
+            compiler_params=pltpu.CompilerParams(vmem_limit_bytes=vmem * 1024 * 1024),
             cost_estimate=pl.CostEstimate(
                 flops=rows // ROWS * steps * 8_000_000, bytes_accessed=8 * rows * LANES, transcendentals=0
             ),
@@ -612,7 +703,7 @@
         padded = pltpu.VMEM((pack.slabs, freq_count + 2 * PAD, LANES), jnp.float32)
         plain = pltpu.VMEM((pack.slabs, freq_count, LANES), jnp.float32)
         column = pltpu.VMEM((freq_count, LANES), jnp.float32)
-        return [padded, padded, padded, plain, plain, column, column]
+        return [padded, padded, padded, plain, plain, column, column, pltpu.VMEM(table.shape, jnp.float32)]
 
     group_count = lax.axis_size("groups")
     chip_swap = []
@@ -630,55 +721,60 @@
         return lax.ppermute(value, ("groups", "tile"), chip_swap)
 
     one_angles, two_angles = jnp.asarray(one.rows()), jnp.asarray(two.rows())
-    one_own, one_send, two_own, two_send, cross, row = pl.pallas_call(
-        functools.partial(spread_kernel, one, two, freq_count),
-        out_shape=(
-            array(one_rows + ROWS, LANES), array(one_rows + ROWS, LANES),
-            array(two_rows + ROWS, LANES), array(two_rows + ROWS, LANES),
-            array(squeezed, LANES), array(ROWS, LANES),
-        ),
-        in_specs=[smem] + [hbm] * 5,
-        out_specs=(vmem,) * 6,
-        scratch_shapes=[
-            pltpu.VMEM((freq_count * dir_count, LANES), jnp.float32),
-            pltpu.VMEM((1, LANES), jnp.int32),
-            pltpu.VMEM((2, LANES), jnp.float32),
-            pltpu.VMEM((1, LANES), jnp.int32),
-            pltpu.VMEM(table.shape, jnp.float32),
-            pltpu.VMEM((dir_count, ROWS, LANES), jnp.float32),
-            pltpu.VMEM((dir_count, ROWS, LANES), jnp.float32),
-            pltpu.SemaphoreType.DMA((4 + freq_count // ROWS,)),
-        ],
-        name="spread",
-        **params(1440, 1),
-    )(
-        code, spectrum.reshape(freq_count * dir_count, cell_count), sea_mask,
-        wind.reshape(2, cell_count), card_deal, table,
-    )
+    flat = spectrum.reshape(freq_count * dir_count, cell_count)
+    whole = pltpu.VMEM((freq_count * dir_count, LANES), jnp.float32)
+    chunks = pltpu.SemaphoreType.DMA((freq_count // ROWS,))
+    one_own, one_send = pl.pallas_call(
+        functools.partial(near_kernel, one, freq_count),
+        out_shape=(array(one_rows, LANES), array(one_rows, LANES)),
+        in_specs=[hbm],
+        out_specs=(vmem,) * 2,
+        scratch_shapes=[whole, chunks],
+        name="near",
+        **params(1440, 1, 53),
+    )(flat)
+    row, own_aux, send_aux = pl.pallas_call(
+        functools.partial(aux_kernel, one, two),
+        out_shape=(array(ROWS, LANES), array(2 * ROWS, LANES), array(2 * ROWS, LANES)),
+        in_specs=[vmem] * 3,
+        out_specs=(vmem,) * 3,
+        name="aux",
+        **params(80, 1),
+    )(sea_mask, wind.reshape(2, cell_count), card_deal)
     one_got = to_pair(one_send)
+    got_aux = to_pair(send_aux)
+    two_own, two_send, cross = pl.pallas_call(
+        functools.partial(coast_kernel, two, freq_count),
+        out_shape=(array(two_rows, LANES), array(two_rows, LANES), array(squeezed, LANES)),
+        in_specs=[smem, hbm, vmem],
+        out_specs=(vmem,) * 3,
+        scratch_shapes=[whole, chunks],
+        name="coast",
+        **params(1440, 1, 53),
+    )(code, flat, row)
     cross_got = to_next(cross)
     two_got = to_pair(two_send)
     one_state, one_column = pl.pallas_call(
         functools.partial(one_kernel, one, freq_count, False),
         out_shape=(array(one_rows + ROWS, LANES), array(freq_count, LANES)),
-        in_specs=[vmem] * 4,
+        in_specs=[vmem] * 7,
         out_specs=(vmem,) * 2,
         scratch_shapes=scratch(one),
         name="first_one",
         **params(one_rows),
-    )(table, one_angles, one_own, one_got)
+    )(table, one_angles, row, one_own, one_got, own_aux, got_aux)
     column_got = to_pair(one_column)
     two_state, two_column, pair, cross = pl.pallas_call(
         functools.partial(two_kernel, two, freq_count, slot_count, False),
         out_shape=(
             array(two_rows + ROWS, LANES), array(freq_count, LANES), array(squeezed, LANES), array(squeezed, LANES),
         ),
-        in_specs=[smem] + [vmem] * 6,
+        in_specs=[smem] + [vmem] * 8,
         out_specs=(vmem,) * 4,
         scratch_shapes=scratch(two),
         name="first_two",
         **params(two_rows),
-    )(code, table, two_angles, row, two_own, two_got, cross_got)
+    )(code, table, two_angles, row, two_own, two_got, own_aux, got_aux, cross_got)
     cross_got = to_next(cross)
     pair_got = to_pair(pair)
     one_state, one_energy = pl.pallas_call(
@@ -701,19 +797,19 @@
         **params(two_rows),
     )(code, table, two_angles, row, two_state, pair_got, cross_got, one_column, one_energy)
     two_got = to_pair(two_state)
-    out = pl.pallas_call(
-        functools.partial(gather_kernel, one, two, freq_count),
-        out_shape=array(freq_count * dir_count, LANES),
-        in_specs=[vmem] * 5,
-        out_specs=vmem,
-        name="gather",
-        **params(1440, 1),
-    )(row, one_state, one_got, two_state, two_got)
     shared = lax.all_to_all(
         energy.reshape(tile_count, 1, LANES), "tile", split_axis=0, concat_axis=0, tiled=True
     )
-    card_energy = jnp.sum(shared, axis=(0, 1))[:slot_count]
-    return out.reshape(freq_count, dir_count, row_count, row_width), card_energy
+    out, card_energy = pl.pallas_call(
+        functools.partial(gather_kernel, one, two, freq_count),
+        out_shape=(array(freq_count * dir_count, LANES), array(1, slot_count)),
+        in_specs=[vmem] * 6,
+        out_specs=(hbm, vmem),
+        scratch_shapes=[whole, chunks],
+        name="gather",
+        **params(1440, 1),
+    )(row, one_state, one_got, two_state, two_got, shared.reshape(tile_count, LANES))
+    return out.reshape(freq_count, dir_count, row_count, row_width), card_energy.reshape(slot_count)
 
 
 def solution(mesh):

time: 44 us -> 40.5 us (0.920)
  local copies, waits for them, and re-layouts: 2.7 us -> 0.17 us
  Pallas kernels: 22.4 us -> 21.8 us
  starting transfers between devices: 5.95 us -> 6.51 us
  other arithmetic: 0.54 us -> 0 us
    unnamed x16 -> x12, local copies, waits for them, and re-layouts: 2.7 us -> 0.17 us
    reduce_sum x1 -> x0, other arithmetic: 0.54 us -> none  [shards(): card_energy = jnp.sum(shared, axis=(0, 1))[:slot_count]]
    ppermute x6 -> x7, starting transfers between devices: 1.9 us -> 2.41 us  [to_pair(): return lax.ppermute(value, 'tile', [(i, i ^ 1) for i in range(tile_count)])]
    pallas_call x1, Pallas kernels: 4.78 us -> 4.3 us  [shards(): pl.pallas_call(functools.partial(one_kernel, one, freq_count, False), out...]
    pallas_call x1, Pallas kernels: 4.84 us -> 4.38 us  [shards(): pl.pallas_call(functools.partial(one_kernel, one, freq_count, True), out_...]
    pallas_call x1 -> x3, Pallas kernels: 4.18 us -> 3.89 us  [the longest x1 2.26 us: shards(): pl.pallas_call(functools.partial(near_kernel, one, freq_count), out_shape...]
  transfers between devices with their start and end apart: 8 -> 9, of which waited for: 0 -> 0; matrix products, arithmetic and copies ran while one was open for 1% -> 0% of each run, Pallas kernels for 38% -> 44%
where the time goes in v4:
time: 40.5 us; the launch traced here: 40.3 us
  Pallas kernels  21.8 us (54%)
  blocking collectives  11.1 us (27%)
  starting transfers between devices  6.51 us (16%)
  between operations  0.73 us (2%)
    all_to_all x1, blocking collectives, shards(): lax.all_to_all(energy.reshape(tile_count, 1, LANES), 'tile', split_axis=0...  11.1 us
    pallas_call x2, Pallas kernels, shards(): pl.pallas_call(functools.partial(two_kernel, two, freq_count, slot_count,...  7.26 us
    pallas_call x1, Pallas kernels, shards(): pl.pallas_call(functools.partial(one_kernel, one, freq_count, True), out_...  4.38 us
    pallas_call x1, Pallas kernels, shards(): pl.pallas_call(functools.partial(one_kernel, one, freq_count, False), out...  4.3 us
    ppermute x2, starting transfers between devices, to_next(): return lax.ppermute(value, ('groups', 'tile'), chip_swap)  4.1 us
    ppermute x7, starting transfers between devices, to_pair(): return lax.ppermute(value, 'tile', [(i, i ^ 1) for i in range(tile_count)])  2.41 us
    pallas_call x1, Pallas kernels, shards(): pl.pallas_call(functools.partial(near_kernel, one, freq_count), out_shape...  2.26 us
    pallas_call x1, Pallas kernels, shards(): pl.pallas_call(functools.partial(gather_kernel, one, two, freq_count), ou...  1.98 us
  transfers between devices with their start and end apart: 9, of which 0 were waited for; matrix products, arithmetic and copies ran while one was open for 0% of the time, Pallas kernels for 44%

profile of v4, /device:TPU:0, one launch (start us, length us, event | category | flops | bytes accessed | tf_op | source)
XLA Modules:
  0.0 40.3 jit_solution(11875302009656087948)
XLA Ops:
  0.6 2.3 %near.1 = (f32[480,128]{1,0:T(8,128)S(1)}, f32[480,128]{1,0:T(8,128)S(1)}) custom-call(f32[1440,128]{1,0:T(8,128)} %bitcast.12), custom_call_target="tpu_custom_call" | custom-call | flops 1440000000 | bytes 1474560 | tf_op jit(solution)/shard_map/near/pallas_call | solution.py:727
  2.9 0.0 copy-start.2
  2.9 0.0 copy-start
  2.9 0.0 copy-start.1
  2.9 0.5 %collective-permute-start = (f32[480,128]{1,0:T(8,128)S(1)}, f32[480,128]{1,0:T(8,128)S(1)}, u32[]{:S(2)}, u32[]{:S(2)}) collective-permute-start(f32[480,128]{1,0:T(8,128)S(1)} %get-tuple-element.24), channel_id=1, source_target_pairs={{0,1},{1,0},{2,3},{3,2},{4,5},{5,4},{6,7},{7,6},{8,9},{9,8},{10,11... | collective-permute-start | bytes 737288 | tf_op jit(solution)/shard_map/ppermute | solution.py:718
  3.4 0.1 copy-done.2
  3.6 0.0 copy-done
  3.6 0.0 copy-done.1
  3.6 0.1 aux.1
  3.7 0.5 %collective-permute-start.1 = (f32[16,128]{1,0:T(8,128)S(1)}, f32[16,128]{1,0:T(8,128)S(1)}, u32[]{:S(2)}, u32[]{:S(2)}) collective-permute-start(f32[16,128]{1,0:T(8,128)S(1)} %get-tuple-element.26), channel_id=1, source_target_pairs={{0,1},{1,0},{2,3},{3,2},{4,5},{5,4},{6,7},{7,6},{8,9},{9,8},{10,11... | collective-permute-start | bytes 24584 | tf_op jit(solution)/shard_map/ppermute | solution.py:718
  4.2 0.0 copy-start.3
  4.2 0.0 copy-start.5
  4.2 1.6 %coast.1 = (f32[360,128]{1,0:T(8,128)S(1)}, f32[360,128]{1,0:T(8,128)S(1)}, f32[96,128]{1,0:T(8,128)S(1)}) custom-call(s32[1]{0:T(128)} %bitcast.2.code_ref, f32[1440,128]{1,0:T(8,128)} %bitcast.13, f32[8,128]{1,0:T(8,128)S(1)} %get-tuple-element.22.refs_0_.row_ref), custom_call_target="tpu_custom_call" | custom-call | flops 1440000000 | bytes 1474560 | tf_op jit(solution)/shard_map/coast/pallas_call | solution.py:746
  5.8 2.6 %collective-permute-start.3 = (f32[96,128]{1,0:T(8,128)S(1)}, f32[96,128]{1,0:T(8,128)S(1)}, u32[]{:S(2)}, u32[]{:S(2)}) collective-permute-start(f32[96,128]{1,0:T(8,128)S(1)} %get-tuple-element.30), channel_id=1, source_target_pairs={{0,16},{1,2},{2,1},{3,4},{4,3},{5,6},{6,5},{7,8},{8,7},{9,10},{10,... | collective-permute-start | bytes 147464 | tf_op jit(solution)/shard_map/ppermute | solution.py:721
  8.4 0.1 collective-permute-start.2
  8.5 0.0 collective-permute-done.1.refs_4_.refs_3_
  8.5 0.0 collective-permute-done.refs_2_
  8.5 0.0 copy-done.3
  8.5 0.0 copy-done.5
  8.5 0.0 copy-start.4
  8.6 4.3 %first_one.1 = (f32[488,128]{1,0:T(8,128)S(1)}, f32[40,128]{1,0:T(8,128)S(1)}) custom-call(f32[5,40,128]{2,1,0:T(8,128)S(1)} %copy-done.5, f32[4,12,8,128]{3,2,1,0:T(8,128)S(1)} %copy-done.3, f32[8,128]{1,0:T(8,128)S(1)} %get-tuple-element.22.refs_0_.row_ref, f32[480,128]{1,0:T(8,128)S(1)} %get-tuple-element.23.refs_1_, ...), custom_call_target="tpu_custom_call" | custom-call | flops 3840000000 | bytes 491520 | tf_op jit(solution)/shard_map/first_one/pallas_call | solution.py:757
  12.9 0.4 %collective-permute-start.4 = (f32[40,128]{1,0:T(8,128)S(1)}, f32[40,128]{1,0:T(8,128)S(1)}, u32[]{:S(2)}, u32[]{:S(2)}) collective-permute-start(f32[40,128]{1,0:T(8,128)S(1)} %get-tuple-element.32.refs_3_), channel_id=1, source_target_pairs={{0,1},{1,0},{2,3},{3,2},{4,5},{5,4},{6,7},{7,6},{8,9},{9,8},{10,11... | collective-permute-start | bytes 61448 | tf_op jit(solution)/shard_map/ppermute | solution.py:718
  13.3 0.0 collective-permute-done.3.refs_4_
  13.3 0.0 collective-permute-done.2.refs_1_
  13.3 0.0 copy-done.4
  13.3 3.7 %first_two.1 = (f32[368,128]{1,0:T(8,128)S(1)}, f32[40,128]{1,0:T(8,128)S(1)}, f32[96,128]{1,0:T(8,128)S(1)}, f32[96,128]{1,0:T(8,128)S(1)}) custom-call(s32[1]{0:T(128)} %bitcast.2.code_ref, f32[5,40,128]{2,1,0:T(8,128)S(1)} %copy-done.5, f32[4,9,8,128]{3,2,1,0:T(8,128)S(1)} %copy-done.4, f32[8,128]{1,0:T(8,128)S(1)} %get-tuple-element.22.refs_0_.row_ref, ...), custom_call_target="tpu_custom_call" | custom-call | flops 2880000000 | bytes 368640 | tf_op jit(solution)/shard_map/first_two/pallas_call | solution.py:767
  17.0 0.2 collective-permute-start.6
  17.2 1.5 %collective-permute-start.7 = (f32[96,128]{1,0:T(8,128)S(1)}, f32[96,128]{1,0:T(8,128)S(1)}, u32[]{:S(2)}, u32[]{:S(2)}) collective-permute-start(f32[96,128]{1,0:T(8,128)S(1)} %get-tuple-element.36), channel_id=1, source_target_pairs={{0,16},{1,2},{2,1},{3,4},{4,3},{5,6},{6,5},{7,8},{8,7},{9,10},{10,... | collective-permute-start | bytes 147464 | tf_op jit(solution)/shard_map/ppermute | solution.py:721
  18.7 0.0 collective-permute-done.4.refs_3_
  18.7 4.4 %second_one.1 = (f32[480,128]{1,0:T(8,128)S(1)}, f32[8,128]{1,0:T(8,128)S(1)}) custom-call(f32[5,40,128]{2,1,0:T(8,128)S(1)} %copy-done.5, f32[4,12,8,128]{3,2,1,0:T(8,128)S(1)} %copy-done.3, f32[8,128]{1,0:T(8,128)S(1)} %get-tuple-element.22.refs_0_.row_ref, f32[488,128]{1,0:T(8,128)S(1)} %get-tuple-element.27.refs_1_, ...), custom_call_target="tpu_custom_call" | custom-call | flops 3840000000 | bytes 491520 | tf_op jit(solution)/shard_map/second_one/pallas_call | solution.py:780
  23.1 0.2 collective-permute-start.5
  23.3 0.0 collective-permute-done.6.refs_1_
  23.3 0.0 collective-permute-done.7.refs_2_
  23.3 3.6 %second_two.1 = (f32[360,128]{1,0:T(8,128)S(1)}, f32[16,128]{1,0:T(8,128)S(1)}) custom-call(s32[1]{0:T(128)} %bitcast.2.code_ref, f32[5,40,128]{2,1,0:T(8,128)S(1)} %copy-done.5, f32[4,9,8,128]{3,2,1,0:T(8,128)S(1)} %copy-done.4, f32[8,128]{1,0:T(8,128)S(1)} %get-tuple-element.22.refs_0_.row_ref, f32[368,128]{1,0:T(8,128)S(1)} %get-tuple-element.34.refs_0_, ...), custom_call_target="tpu_custom_call" | custom-call | flops 2880000000 | bytes 368640 | tf_op jit(solution)/shard_map/second_two/pallas_call | solution.py:790
  26.9 0.4 collective-permute-start.8
  27.3 11.1 %all_to_all.5 = f32[16,1,128]{2,1,0:T(1,128)S(1)} all-to-all(f32[16,1,128]{2,1,0:T(1,128)S(1)} %bitcast.9), channel_id=1, replica_groups=mesh['groups'=2,'tile'=16] {'tile'}, dimensions={0} | all-to-all | bytes 16384 | tf_op jit(solution)/shard_map/all_to_all | solution.py:800
  38.4 0.0 collective-permute-done.8.two_got
  38.4 0.0 collective-permute-done.5.one_got
  38.4 2.0 %gather.1 = (f32[1440,128]{1,0:T(8,128)}, f32[1,16]{1,0:T(1,128)}) custom-call(f32[8,128]{1,0:T(8,128)S(1)} %get-tuple-element.22.refs_0_.row_ref, f32[480,128]{1,0:T(8,128)S(1)} %get-tuple-element.33.one_ref, f32[480,128]{1,0:T(8,128)S(1)} %collective-permute-done.5.one_got, f32[360,128]{1,0:T(8,128)S(1)} %get-tuple-element.38.two_ref, ...), custom_call_target="tpu_custom_call" | custom-call | flops 1440000000 | bytes 1474560 | tf_op jit(solution)/shard_map/gather/pallas_call | solution.py:803
Async XLA Ops:
  2.9 0.7 %copy-start.2 = (s32[1,128]{1,0:T(1,128)S(1)}, s32[1,128]{1,0:T(1,128)}, u32[]{:S(2)}) copy-start(s32[1,128]{1,0:T(1,128)} %deal_ref.1) | copy-start | bytes 1540
  2.9 0.7 %copy-start = (f32[2,1,128]{2,1,0:T(1,128)S(1)}, f32[2,1,128]{2,1,0:T(1,128)}, u32[]{:S(2)}) copy-start(f32[2,1,128]{2,1,0:T(1,128)} %param.10) | copy-start | bytes 3076
  2.9 0.7 %copy-start.1 = (s32[1,128]{1,0:T(1,128)S(1)}, s32[1,128]{1,0:T(1,128)}, u32[]{:S(2)}) copy-start(s32[1,128]{1,0:T(1,128)} %mask_ref.1) | copy-start | bytes 1540
  2.9 5.6 %collective-permute-start = (f32[480,128]{1,0:T(8,128)S(1)}, f32[480,128]{1,0:T(8,128)S(1)}, u32[]{:S(2)}, u32[]{:S(2)}) collective-permute-start(f32[480,128]{1,0:T(8,128)S(1)} %get-tuple-element.24), channel_id=1, source_target_pairs={{0,1},{1,0},{2,3},{3,2},{4,5},{5,4},{6,7},{7,6},{8,9},{9,8},{10,11... | collective-permute-start | bytes 737288 | tf_op jit(solution)/shard_map/ppermute | solution.py:718
  3.7 4.8 %collective-permute-start.1 = (f32[16,128]{1,0:T(8,128)S(1)}, f32[16,128]{1,0:T(8,128)S(1)}, u32[]{:S(2)}, u32[]{:S(2)}) collective-permute-start(f32[16,128]{1,0:T(8,128)S(1)} %get-tuple-element.26), channel_id=1, source_target_pairs={{0,1},{1,0},{2,3},{3,2},{4,5},{5,4},{6,7},{7,6},{8,9},{9,8},{10,11... | collective-permute-start | bytes 24584 | tf_op jit(solution)/shard_map/ppermute | solution.py:718
  4.2 4.3 %copy-start.3 = (f32[4,12,8,128]{3,2,1,0:T(8,128)S(1)}, f32[4,12,8,128]{3,2,1,0:T(8,128)}, u32[]{:S(2)}) copy-start(f32[4,12,8,128]{3,2,1,0:T(8,128)} %constant.28.clone.angle_ref) | copy-start | bytes 589828
  4.2 4.3 %copy-start.5 = (f32[5,40,128]{2,1,0:T(8,128)S(1)}, f32[5,40,128]{2,1,0:T(8,128)}, u32[]{:S(2)}) copy-start(f32[5,40,128]{2,1,0:T(8,128)} %constant.27.clone.table_ref) | copy-start | bytes 307204
  5.8 7.5 %collective-permute-start.3 = (f32[96,128]{1,0:T(8,128)S(1)}, f32[96,128]{1,0:T(8,128)S(1)}, u32[]{:S(2)}, u32[]{:S(2)}) collective-permute-start(f32[96,128]{1,0:T(8,128)S(1)} %get-tuple-element.30), channel_id=1, source_target_pairs={{0,16},{1,2},{2,1},{3,4},{4,3},{5,6},{6,5},{7,8},{8,7},{9,10},{10,... | collective-permute-start | bytes 147464 | tf_op jit(solution)/shard_map/ppermute | solution.py:721
  8.4 4.9 %collective-permute-start.2 = (f32[360,128]{1,0:T(8,128)S(1)}, f32[360,128]{1,0:T(8,128)S(1)}, u32[]{:S(2)}, u32[]{:S(2)}) collective-permute-start(f32[360,128]{1,0:T(8,128)S(1)} %get-tuple-element.29), channel_id=1, source_target_pairs={{0,1},{1,0},{2,3},{3,2},{4,5},{5,4},{6,7},{7,6},{8,9},{9,8},{10,11... | collective-permute-start | bytes 552968 | tf_op jit(solution)/shard_map/ppermute | solution.py:718
  8.5 4.8 %copy-start.4 = (f32[4,9,8,128]{3,2,1,0:T(8,128)S(1)}, f32[4,9,8,128]{3,2,1,0:T(8,128)}, u32[]{:S(2)}) copy-start(f32[4,9,8,128]{3,2,1,0:T(8,128)} %constant.29.clone.angle_ref) | copy-start | bytes 442372
  12.9 5.9 %collective-permute-start.4 = (f32[40,128]{1,0:T(8,128)S(1)}, f32[40,128]{1,0:T(8,128)S(1)}, u32[]{:S(2)}, u32[]{:S(2)}) collective-permute-start(f32[40,128]{1,0:T(8,128)S(1)} %get-tuple-element.32.refs_3_), channel_id=1, source_target_pairs={{0,1},{1,0},{2,3},{3,2},{4,5},{5,4},{6,7},{7,6},{8,9},{9,8},{10,11... | collective-permute-start | bytes 61448 | tf_op jit(solution)/shard_map/ppermute | solution.py:718
  17.0 6.3 %collective-permute-start.6 = (f32[96,128]{1,0:T(8,128)S(1)}, f32[96,128]{1,0:T(8,128)S(1)}, u32[]{:S(2)}, u32[]{:S(2)}) collective-permute-start(f32[96,128]{1,0:T(8,128)S(1)} %get-tuple-element.35), channel_id=1, source_target_pairs={{0,1},{1,0},{2,3},{3,2},{4,5},{5,4},{6,7},{7,6},{8,9},{9,8},{10,11... | collective-permute-start | bytes 147464 | tf_op jit(solution)/shard_map/ppermute | solution.py:718
  17.2 6.1 %collective-permute-start.7 = (f32[96,128]{1,0:T(8,128)S(1)}, f32[96,128]{1,0:T(8,128)S(1)}, u32[]{:S(2)}, u32[]{:S(2)}) collective-permute-start(f32[96,128]{1,0:T(8,128)S(1)} %get-tuple-element.36), channel_id=1, source_target_pairs={{0,16},{1,2},{2,1},{3,4},{4,3},{5,6},{6,5},{7,8},{8,7},{9,10},{10,... | collective-permute-start | bytes 147464 | tf_op jit(solution)/shard_map/ppermute | solution.py:721
  23.1 15.3 %collective-permute-start.5 = (f32[480,128]{1,0:T(8,128)S(1)}, f32[480,128]{1,0:T(8,128)S(1)}, u32[]{:S(2)}, u32[]{:S(2)}) collective-permute-start(f32[480,128]{1,0:T(8,128)S(1)} %get-tuple-element.33.one_ref), channel_id=1, source_target_pairs={{0,1},{1,0},{2,3},{3,2},{4,5},{5,4},{6,7},{7,6},{8,9},{9,8},{10,11... | collective-permute-start | bytes 737288 | tf_op jit(solution)/shard_map/ppermute | solution.py:718
  26.9 11.5 %collective-permute-start.8 = (f32[360,128]{1,0:T(8,128)S(1)}, f32[360,128]{1,0:T(8,128)S(1)}, u32[]{:S(2)}, u32[]{:S(2)}) collective-permute-start(f32[360,128]{1,0:T(8,128)S(1)} %get-tuple-element.38.two_ref), channel_id=1, source_target_pairs={{0,1},{1,0},{2,3},{3,2},{4,5},{5,4},{6,7},{7,6},{8,9},{9,8},{10,11... | collective-permute-start | bytes 552968 | tf_op jit(solution)/shard_map/ppermute | solution.py:718
